TPU v7x, 512 devices: a whole 4x4x16 slice. The times are simulated.
512 devices in a mesh: enc: 8 (over x, core), llm: 4 (over y), sp: 16 (over z).
Axes of the slice: x: 4, y: 4, z: 16, core: 2. Of those that a mesh axis runs over, the one named last changes fastest.
Arguments:
- text_qkv: bfloat16 [8, 4, 2048, 5120], P('enc', 'llm', 'sp'), may hold values from -12 to 12
- segments: int32 [8, 4, 2048], P('enc', 'llm', 'sp'), may hold values from 0 to 31, never falling along the last dimension, each value on 1 to 256 neighbouring positions
- image_qkv: bfloat16 [8, 4, 16, 64, 5120], P('enc', 'llm', 'sp'), may hold values from -6 to 6
- patch_counts: int32 [8, 4, 16, 2], P('enc', 'llm', 'sp'), may hold values from 8 to 32, as said below
- image_dest: int32 [8, 4, 16, 64], P('enc', 'llm', 'sp'), may hold values from 0 to 31, as said below
- image_offset: int32 [8, 4, 16, 64], P('enc', 'llm', 'sp'), may hold values from 0 to 127, as said below
- output_cotangent: bfloat16 [8, 4, 2048, 4096], P('enc', 'llm', 'sp'), may hold values from -6 to 6
Outputs:
- text_grad: bfloat16 [8, 4, 2048, 5120], P('enc', 'llm', 'sp')
- image_grad: bfloat16 [8, 4, 16, 64, 5120], P('enc', 'llm', 'sp')
Inputs may be any that keep to these rules, and one draw needn't show every extreme that they name: `patch_counts`: each encoder shard has 2 images, one of exactly 32 patches; rows past an image's count are padding and their entries are not used. `image_dest`: from each encoder shard at most 4 live rows go to any one slab, and exactly 4 go to one slab that is drawn separately for each shard, so it may differ from shard to shard. `image_offset`: live rows that go to the same slab and sp index never share a position.
All inputs are finite; a program needn't handle non-finite values.
Results may differ from a plain program's by a relative error of at most 0.014.
Values may be sent and summed in bfloat16 or wider, within the bound.
A program may use at most 64 MiB of HBM per device.

v0:
```python
import jax
import jax.numpy as jnp
from jax import lax
from jax.sharding import PartitionSpec as P

QUERY_HEADS = 32
KEY_VALUE_HEADS = 4
HEAD_SIZE = 128
SEG_MAX = 256


NEG_FILL = -1e30


def passed_along(value, axis, by):
    count = lax.axis_size(axis)
    pairs = [(i, i + by) for i in range(count) if 0 <= i + by < count]
    return lax.ppermute(value, axis, pairs)


def masked_logits(queries_four, keys_four, visible):
    logits = jnp.einsum(
        "qhgd,khd->hgqk", queries_four, keys_four, preferred_element_type=jnp.float32
    ) * HEAD_SIZE ** (-0.5)
    return jnp.where(visible[None, None], logits, NEG_FILL)


def body(text_qkv, segments, image_qkv, patch_counts, image_dest, image_offset, output_cotangent):
    token_per_shard = text_qkv.shape[2]
    width_per_row = text_qkv.shape[3]
    q_width = QUERY_HEADS * HEAD_SIZE
    enc_size = lax.axis_size("enc")
    llm_size = lax.axis_size("llm")
    senders = enc_size * llm_size
    capacity = token_per_shard // senders
    slot_total = senders * capacity
    image_rows = image_qkv[0, 0, 0]
    img_rows = image_rows.shape[0]
    image_total = patch_counts.shape[3]
    per_image = img_rows // image_total
    image_counts = patch_counts[0, 0, 0]
    row_ids = jnp.arange(img_rows, dtype=jnp.int32)
    owner_match = (row_ids // per_image)[:, None] == jnp.arange(image_total, dtype=jnp.int32)[
        None, :
    ]
    row_count = jnp.sum(jnp.where(owner_match, image_counts[None, :], 0), axis=1)
    is_live = row_ids % per_image < row_count
    destination = image_dest[0, 0, 0]
    offsets = image_offset[0, 0, 0]
    earlier = (
        (destination[:, None] == destination[None, :])
        & is_live[None, :]
        & (row_ids[None, :] < row_ids[:, None])
    )
    rank_within = jnp.sum(earlier.astype(jnp.int32), axis=1)
    slot_index = jnp.where(is_live, destination * capacity + rank_within, -1)
    packing = slot_index[None, :] == jnp.arange(slot_total, dtype=jnp.int32)[:, None]
    packing_b = packing.astype(jnp.bfloat16)
    outgoing = jnp.dot(packing_b, image_rows, preferred_element_type=jnp.float32).astype(
        jnp.bfloat16
    )
    slot_marks = jnp.sum(jnp.where(packing, offsets[None, :] + 1, 0), axis=1)
    arrived, arrived_marks = (
        lax.all_to_all(
            outgoing.reshape(senders, capacity, width_per_row),
            ("enc", "llm"),
            split_axis=0,
            concat_axis=0,
            tiled=True,
        ),
        lax.all_to_all(
            slot_marks.reshape(senders, capacity),
            ("enc", "llm"),
            split_axis=0,
            concat_axis=0,
            tiled=True,
        ),
    )
    arrived = arrived.reshape(slot_total, width_per_row)
    arrived_marks = arrived_marks.reshape(slot_total)
    placing = arrived_marks[None, :] == jnp.arange(token_per_shard, dtype=jnp.int32)[:, None] + 1
    placing_b = placing.astype(jnp.bfloat16)
    is_image = jnp.any(placing, axis=1)
    landed = jnp.dot(placing_b, arrived, preferred_element_type=jnp.float32).astype(jnp.bfloat16)
    mixed = jnp.where(is_image[:, None], landed, text_qkv[0, 0])
    query_rows = mixed[:, :q_width]
    key_value = mixed[:, q_width:]
    query_seg = segments[0, 0]
    halo_depth = (SEG_MAX + token_per_shard - 2) // token_per_shard
    first_pos = lax.axis_index("sp") * token_per_shard
    halo_parts = []
    seg_parts = []
    for distance in range(halo_depth, 0, -1):
        received, received_seg = passed_along((key_value, query_seg), "sp", distance)
        halo_parts.append(received)
        seg_parts.append(received_seg)
    every_key = jnp.concatenate(halo_parts + [key_value], axis=0)
    key_seg = jnp.concatenate(seg_parts + [query_seg], axis=0)
    key_number = every_key.shape[0]
    key_pos = first_pos - halo_depth * token_per_shard + jnp.arange(key_number, dtype=jnp.int32)
    query_pos = first_pos + jnp.arange(token_per_shard, dtype=jnp.int32)
    visible = (
        (query_seg[:, None] == key_seg[None, :])
        & (key_pos[None, :] <= query_pos[:, None])
        & (key_pos[None, :] >= 0)
    )
    query_groups = QUERY_HEADS // KEY_VALUE_HEADS
    queries_four = query_rows.reshape(token_per_shard, KEY_VALUE_HEADS, query_groups, HEAD_SIZE)
    keys_four = every_key[:, : KEY_VALUE_HEADS * HEAD_SIZE].reshape(
        key_number, KEY_VALUE_HEADS, HEAD_SIZE
    )
    values_four = every_key[:, KEY_VALUE_HEADS * HEAD_SIZE :].reshape(
        key_number, KEY_VALUE_HEADS, HEAD_SIZE
    )
    logits = masked_logits(queries_four, keys_four, visible)
    top = jnp.max(logits, axis=-1, keepdims=True)
    log_total = top + jnp.log(jnp.sum(jnp.exp(logits - top), axis=-1, keepdims=True))
    probs = jnp.exp(logits - log_total)
    probs_b = probs.astype(jnp.bfloat16)
    attended = jnp.einsum(
        "hgqk,khd->qhgd", probs_b, values_four, preferred_element_type=jnp.float32
    ).astype(jnp.bfloat16)
    gradient_four = output_cotangent[0, 0].reshape(
        token_per_shard, KEY_VALUE_HEADS, query_groups, HEAD_SIZE
    )
    delta = jnp.sum(gradient_four.astype(jnp.float32) * attended.astype(jnp.float32), axis=-1)
    delta = jnp.transpose(delta, (1, 2, 0))[..., None]
    value_gradient = jnp.einsum(
        "hgqk,qhgd->khd", probs_b, gradient_four, preferred_element_type=jnp.float32
    )
    grad_probs = jnp.einsum(
        "qhgd,khd->hgqk", gradient_four, values_four, preferred_element_type=jnp.float32
    )
    grad_logits = (probs * (grad_probs - delta) * HEAD_SIZE ** (-0.5)).astype(jnp.bfloat16)
    grad_queries = jnp.einsum(
        "hgqk,khd->qhgd", grad_logits, keys_four, preferred_element_type=jnp.float32
    )
    grad_queries = grad_queries.astype(jnp.bfloat16).reshape(token_per_shard, q_width)
    key_gradient = jnp.einsum(
        "hgqk,qhgd->khd", grad_logits, queries_four, preferred_element_type=jnp.float32
    )
    key_value_gradient = jnp.concatenate(
        [
            key_gradient.reshape(key_number, KEY_VALUE_HEADS * HEAD_SIZE),
            value_gradient.reshape(key_number, KEY_VALUE_HEADS * HEAD_SIZE),
        ],
        axis=1,
    )
    own_grad = key_value_gradient[halo_depth * token_per_shard :]
    pieces = [
        key_value_gradient[
            (halo_depth - distance)
            * token_per_shard : (halo_depth - distance + 1)
            * token_per_shard
        ]
        for distance in range(1, halo_depth + 1)
    ]
    for distance in range(1, halo_depth + 1):
        own_grad = own_grad + passed_along(
            pieces[distance - 1].astype(jnp.bfloat16), "sp", -distance
        ).astype(jnp.float32)
    grad_slab = jnp.concatenate([grad_queries, own_grad.astype(jnp.bfloat16)], axis=1)
    text_grad = jnp.where(is_image[:, None], jnp.zeros_like(grad_slab), grad_slab)
    returning = jnp.dot(placing_b.T, grad_slab, preferred_element_type=jnp.float32).astype(
        jnp.bfloat16
    )
    returned = lax.all_to_all(
        returning.reshape(senders, capacity, width_per_row),
        ("enc", "llm"),
        split_axis=0,
        concat_axis=0,
        tiled=True,
    )
    returned = returned.reshape(slot_total, width_per_row)
    image_grad = jnp.dot(packing_b.T, returned, preferred_element_type=jnp.float32).astype(
        jnp.bfloat16
    )
    return (
        text_grad.reshape(1, 1, token_per_shard, width_per_row),
        image_grad.reshape(1, 1, 1, img_rows, width_per_row),
    )


def solution(mesh):
    in_specs = (
        P("enc", "llm", "sp", None),
        P("enc", "llm", "sp"),
        P("enc", "llm", "sp", None, None),
        P("enc", "llm", "sp", None),
        P("enc", "llm", "sp", None),
        P("enc", "llm", "sp", None),
        P("enc", "llm", "sp", None),
    )
    out_specs = (P("enc", "llm", "sp", None), P("enc", "llm", "sp", None, None))
    return jax.shard_map(body, mesh=mesh, in_specs=in_specs, out_specs=out_specs, check_vma=False)
```

profile of v0, /device:TPU:64, one launch (start us, length us, event | category | flops | bytes accessed | tf_op | source)
XLA Modules:
  0.0 142.4 jit_solution(7656977955974227678)
XLA Ops:
  4.5 7.3 %all-to-all-start = ((s32[32,1,4]{2,1,0:T(1,128)}), s32[32,1,4]{2,1,0:T(1,128)S(1)}, u32[]{:S(2)}, u32[]{:S(2)}) async-start(s32[32,1,4]{2,1,0:T(1,128)} %bitcast.3), calls=%async_computation | async-start | bytes 32768 | tf_op jit(solution)/shard_map/all_to_all | solution.py:71
  12.5 1.3 reshape.241
  13.9 5.3 %all-to-all-done = s32[32,1,4]{2,1,0:T(1,128)S(1)} async-done(((s32[32,1,4]{2,1,0:T(1,128)}), s32[32,1,4]{2,1,0:T(1,128)S(1)}, u32[]{:S(2)}, u32[]{:S(2)}) %all-to-all-start) | async-done | bytes 544 | tf_op jit(solution)/shard_map/all_to_all | solution.py:71
  19.1 4.0 %all-to-all-start.1 = ((bf16[32,4,5120]{2,1,0:T(4,128)(2,1)}), bf16[32,4,5120]{2,1,0:T(4,128)(2,1)S(1)}, u32[]{:S(2)}, u32[]{:S(2)}) async-start(bf16[32,4,5120]{2,1,0:T(4,128)(2,1)} %reshape.241), calls=%async_computation.1 | async-start | bytes 2621440 | tf_op jit(solution)/shard_map/all_to_all | solution.py:64
  23.1 3.8 %collective-permute-start.3 = (s32[128]{0:T(128)S(1)}, s32[128]{0:T(128)S(1)}, u32[]{:S(2)}, u32[]{:S(2)}) collective-permute-start(s32[128]{0:T(128)S(1)} %bitcast.89), channel_id=1, source_target_pairs={{0,1},{1,2},{2,3},{3,4},{4,5},{5,6},{6,7},{7,8},{8,9},{9,10},{10,1... | collective-permute-start | bytes 1544 | tf_op jit(solution)/shard_map/ppermute | solution.py:18
  26.9 6.4 %collective-permute-start.2 = (s32[128]{0:T(128)S(1)}, s32[128]{0:T(128)S(1)}, u32[]{:S(2)}, u32[]{:S(2)}) collective-permute-start(s32[128]{0:T(128)S(1)} %bitcast.90), channel_id=1, source_target_pairs={{0,2},{1,3},{2,4},{3,5},{4,6},{5,7},{6,8},{7,9},{8,10},{9,11},{10,... | collective-permute-start | bytes 1544 | tf_op jit(solution)/shard_map/ppermute | solution.py:18
  33.3 1.3 copy.60
  36.4 6.5 %all-to-all-done.1 = bf16[32,4,5120]{2,1,0:T(4,128)(2,1)S(1)} async-done(((bf16[32,4,5120]{2,1,0:T(4,128)(2,1)}), bf16[32,4,5120]{2,1,0:T(4,128)(2,1)S(1)}, u32[]{:S(2)}, u32[]{:S(2)}) %all-to-all-start.1) | async-done | bytes 1310752 | tf_op jit(solution)/shard_map/all_to_all | solution.py:64
  43.3 1.9 %fusion.3 = bf16[128,5120]{1,0:T(8,128)(2,1)S(1)} fusion(bf16[128,5120]{1,0:T(8,128)(2,1)S(1)} %reshape.242, bf16[1,1,128,5120]{3,2,1,0:T(8,128)(2,1)} %param.7, pred[128]{0:T(512)(128)(4,1)S(1)} %compare_reduce_fusion, s32[128]{0:T(128)S(1)} %eq.84, s32[128]{0:T(128)S(1)} %iota_add_fusion.2), kind=kOutput, calls=%fused_computation.10 | convolution fusion | flops 169099264 | bytes 3933312 | tf_op jit(solution)/shard_map/dot_general | solution.py:84
  45.2 3.8 %collective-permute-start.1 = (bf16[128,1024]{1,0:T(8,128)(2,1)S(1)}, bf16[128,1024]{1,0:T(8,128)(2,1)S(1)}, u32[]{:S(2)}, u32[]{:S(2)}) collective-permute-start(bf16[128,1024]{1,0:T(8,128)(2,1)S(1)} %slice.30), channel_id=1, source_target_pairs={{0,1},{1,2},{2,3},{3,4},{4,5},{5,6},{6,7},{7,8},{8,9},{9,10},{10,1... | collective-permute-start | bytes 786440 | tf_op jit(solution)/shard_map/ppermute | solution.py:18
  49.0 6.6 %collective-permute-start = (bf16[128,1024]{1,0:T(8,128)(2,1)S(1)}, bf16[128,1024]{1,0:T(8,128)(2,1)S(1)}, u32[]{:S(2)}, u32[]{:S(2)}) collective-permute-start(bf16[128,1024]{1,0:T(8,128)(2,1)S(1)} %slice.30), channel_id=1, source_target_pairs={{0,2},{1,3},{2,4},{3,5},{4,6},{5,7},{6,8},{7,9},{8,10},{9,11},{10,... | collective-permute-start | bytes 786440 | tf_op jit(solution)/shard_map/ppermute | solution.py:18
  55.9 4.5 %collective-permute-done.1 = bf16[128,1024]{1,0:T(8,128)(2,1)S(1)} collective-permute-done((bf16[128,1024]{1,0:T(8,128)(2,1)S(1)}, bf16[128,1024]{1,0:T(8,128)(2,1)S(1)}, u32[]{:S(2)}, u32[]{:S(2)}) %collective-permute-start.1) | collective-permute-done | bytes 262176 | tf_op jit(solution)/shard_map/ppermute | solution.py:18
  60.5 5.3 %collective-permute-done = bf16[128,1024]{1,0:T(8,128)(2,1)S(1)} collective-permute-done((bf16[128,1024]{1,0:T(8,128)(2,1)S(1)}, bf16[128,1024]{1,0:T(8,128)(2,1)S(1)}, u32[]{:S(2)}, u32[]{:S(2)}) %collective-permute-start) | collective-permute-done | bytes 262176 | tf_op jit(solution)/shard_map/ppermute | solution.py:18
  67.4 1.4 %fusion.6 = (f32[4,8,128]{2,1,0:T(8,128)S(1)}, f32[4,384,128,8]{2,1,3,0:T(8,128)S(1)}) fusion(pred[128,384]{0,1:T(8,128)(4,1)S(1)} %and_and_fusion, bf16[384,4,128,1]{0,2,3,1:T(8,128)(2,1)S(1)} %copy.78, bf16[128,4,8,128]{3,2,1,0:T(8,128)(2,1)S(1)} %bitcast.78), kind=kOutput, calls=%fused_computation.14 | convolution fusion | flops 407367680 | bytes 7798784 | tf_op jit(solution)/shard_map/qhgd,khd->hgqk/dot_general | solution.py:22
  68.9 1.4 exponential_reduce_fusion
  70.4 1.6 %fusion.20 = f32[4,384,128,1]{1,2,3,0:T(8,128)S(1)} fusion(bf16[128,4,8,128]{0,3,2,1:T(8,128)(2,1)S(1)} %bitcast.84, f32[4,384,128,8]{2,1,3,0:T(8,128)S(1)} %get-tuple-element.7, f32[4,8,128]{2,1,0:T(8,128)S(1)} %log_add_fusion, pred[128,384]{0,1:T(8,128)(4,1)S(1)} %and_and_fusion), kind=kOutput, calls=%fused_computation.40 | convolution fusion | flops 408944640 | bytes 8192000 | tf_op jit(solution)/shard_map/hgqk,qhgd->khd/dot_general | solution.py:128
  72.0 1.9 %fusion.7 = f32[128,4,8]{0,2,1:T(8,128)S(1)} fusion(bf16[128,4,8,128]{0,3,2,1:T(8,128)(2,1)S(1)} %bitcast.85, bf16[384,4,128,1]{0,2,3,1:T(8,128)(2,1)S(1)} %copy-done.5, f32[4,384,128,8]{2,1,3,0:T(8,128)S(1)} %get-tuple-element.7, f32[4,8,128]{2,1,0:T(8,128)S(1)} %log_add_fusion, pred[128,384]{0,1:T(8,128)(4,1)S(1)} %and_and_fusion), kind=kOutput, calls=%fused_computation.16 | convolution fusion | flops 411561984 | bytes 7815168 | tf_op jit(solution)/shard_map/hgqk,khd->qhgd/dot_general | solution.py:120
  73.9 3.6 %fusion.2 = bf16[4,8,128,384]{2,3,1,0:T(8,128)(2,1)} fusion(f32[4,384,128,8]{2,1,3,0:T(8,128)S(1)} %get-tuple-element.7, f32[4,8,128]{2,1,0:T(8,128)S(1)} %bitcast.94, f32[4,8,128]{2,1,0:T(8,128)S(1)} %log_add_fusion, pred[128,384]{0,1:T(8,128)(4,1)S(1)} %and_and_fusion, bf16[384,4,128,1]{0,2,3,1:T(8,128)(2,1)S(1)} %copy-done.5, ...), kind=kOutput, calls=%fused_computation.3 | convolution fusion | flops 413663232 | bytes 10960896 | tf_op jit(solution)/shard_map/qhgd,khd->hgqk/dot_general | solution.py:131
  77.7 5.1 %copy.67 = bf16[4,8,128,384]{3,1,0,2:T(8,128)(2,1)} copy(bf16[4,8,128,384]{2,3,1,0:T(8,128)(2,1)} %fusion.2) | data formatting | bytes 6291456 | tf_op jit(solution)/shard_map/convert_element_type | solution.py:134
  82.8 3.5 %fusion.39 = f32[4,128,384,1]{2,1,0,3:T(8,128)} fusion(bf16[128,4,8,128]{3,2,1,0:T(8,128)(2,1)S(1)} %bitcast.79, bf16[4,8,128,384]{3,1,0,2:T(8,128)(2,1)} %copy.67), kind=kOutput, calls=%fused_computation.75 | convolution fusion | flops 402653184 | bytes 4980736 | tf_op jit(solution)/shard_map/hgqk,qhgd->khd/dot_general | solution.py:139
  86.3 1.4 copy.69
  87.9 2.2 %collective-permute-start.4 = (bf16[128,1024]{1,0:T(8,128)(2,1)S(1)}, bf16[128,1024]{1,0:T(8,128)(2,1)S(1)}, u32[]{:S(2)}, u32[]{:S(2)}) collective-permute-start(bf16[128,1024]{1,0:T(8,128)(2,1)S(1)} %get-tuple-element.2), channel_id=1, source_target_pairs={{1,0},{2,1},{3,2},{4,3},{5,4},{6,5},{7,6},{8,7},{9,8},{10,9},{11,1... | collective-permute-start | bytes 786440 | tf_op jit(solution)/shard_map/ppermute | solution.py:18
  90.1 1.9 %collective-permute-start.5 = (bf16[128,1024]{1,0:T(8,128)(2,1)S(1)}, bf16[128,1024]{1,0:T(8,128)(2,1)S(1)}, u32[]{:S(2)}, u32[]{:S(2)}) collective-permute-start(bf16[128,1024]{1,0:T(8,128)(2,1)S(1)} %get-tuple-element.3), channel_id=1, source_target_pairs={{2,0},{3,1},{4,2},{5,3},{6,4},{7,5},{8,6},{9,7},{10,8},{11,9},{12,... | collective-permute-start | bytes 786440 | tf_op jit(solution)/shard_map/ppermute | solution.py:18
  92.0 1.7 %convolution_convert_fusion.4 = bf16[4,128,8,128]{3,1,2,0:T(8,128)(2,1)S(1)} fusion(bf16[384,4,128,1]{0,2,3,1:T(8,128)(2,1)} %copy-done.2, bf16[4,8,128,384]{2,3,1,0:T(8,128)(2,1)S(1)} %copy-done.1), kind=kOutput, calls=%fused_computation.21 | convolution fusion | flops 403177472 | bytes 4587520 | tf_op jit(solution)/shard_map/hgqk,khd->qhgd/dot_general | solution.py:135
  93.8 7.8 %collective-permute-done.4 = bf16[128,1024]{1,0:T(8,128)(2,1)S(1)} collective-permute-done((bf16[128,1024]{1,0:T(8,128)(2,1)S(1)}, bf16[128,1024]{1,0:T(8,128)(2,1)S(1)}, u32[]{:S(2)}, u32[]{:S(2)}) %collective-permute-start.4) | collective-permute-done | bytes 262176 | tf_op jit(solution)/shard_map/ppermute | solution.py:18
  101.5 10.0 %collective-permute-done.5 = bf16[128,1024]{1,0:T(8,128)(2,1)S(1)} collective-permute-done((bf16[128,1024]{1,0:T(8,128)(2,1)S(1)}, bf16[128,1024]{1,0:T(8,128)(2,1)S(1)}, u32[]{:S(2)}, u32[]{:S(2)}) %collective-permute-start.5) | collective-permute-done | bytes 262176 | tf_op jit(solution)/shard_map/ppermute | solution.py:18
  112.4 1.4 reshape.249
  113.8 4.9 %all-to-all-start.2 = ((bf16[32,4,5120]{2,1,0:T(4,128)(2,1)}), bf16[32,4,5120]{2,1,0:T(4,128)(2,1)S(1)}, u32[]{:S(2)}, u32[]{:S(2)}) async-start(bf16[32,4,5120]{2,1,0:T(4,128)(2,1)} %reshape.249), calls=%async_computation.2 | async-start | bytes 2621440 | tf_op jit(solution)/shard_map/all_to_all | solution.py:167
  118.7 1.3 copy.71
  120.0 2.6 %maximum_select_fusion = bf16[1,1,128,5120]{3,2,1,0:T(8,128)(2,1)} fusion(bf16[1,1,128,1024]{3,2,1,0:T(8,128)(2,1)S(1)} %bitcast.81, bf16[1,1,128,4096]{3,2,1,0:T(8,128)(2,1)} %copy.71, pred[128]{0:T(512)(128)(4,1)S(1)} %compare_reduce_fusion), kind=kLoop, calls=%fused_computation.23 | loop fusion | flops 3276800 | bytes 2621568 | tf_op jit(solution)/shard_map/jit(_where)/select_n | solution.py:163
  122.6 16.0 %all-to-all-done.2 = bf16[32,4,5120]{2,1,0:T(4,128)(2,1)S(1)} async-done(((bf16[32,4,5120]{2,1,0:T(4,128)(2,1)}), bf16[32,4,5120]{2,1,0:T(4,128)(2,1)S(1)}, u32[]{:S(2)}, u32[]{:S(2)}) %all-to-all-start.2) | async-done | bytes 1310752 | tf_op jit(solution)/shard_map/all_to_all | solution.py:167
  139.8 2.5 %fusion.4 = bf16[1,1,1,64,5120]{4,3,2,1,0:T(8,128)(2,1)} fusion(bf16[128,5120]{1,0:T(8,128)(2,1)} %reshape.250, s32[64]{0:T(128)S(1)} %add_select_fusion), kind=kOutput, calls=%fused_computation.12 | convolution fusion | flops 84221952 | bytes 1966336 | tf_op jit(solution)/shard_map/dot_general | solution.py:175
  (53 shorter events, 11.0 us)
Async XLA Ops:
  0.6 11.2 %copy-start = (bf16[1,1,1,64,5120]{4,3,2,1,0:T(8,128)(2,1)S(1)}, bf16[1,1,1,64,5120]{4,3,2,1,0:T(8,128)(2,1)}, u32[]{:S(2)}) copy-start(bf16[1,1,1,64,5120]{4,3,2,1,0:T(8,128)(2,1)} %param.9) | copy-start | bytes 1966084
  4.5 14.6 %all-to-all-start = ((s32[32,1,4]{2,1,0:T(1,128)}), s32[32,1,4]{2,1,0:T(1,128)S(1)}, u32[]{:S(2)}, u32[]{:S(2)}) async-start(s32[32,1,4]{2,1,0:T(1,128)} %bitcast.3), calls=%async_computation | async-start | bytes 32768 | tf_op jit(solution)/shard_map/all_to_all | solution.py:71
  12.5 10.6 %copy-start.6 = (s32[1,1,128]{2,1,0:T(1,128)S(1)}, s32[1,1,128]{2,1,0:T(1,128)}, u32[]{:S(2)}) copy-start(s32[1,1,128]{2,1,0:T(1,128)} %param.8) | copy-start | bytes 1540
  12.5 20.8 %copy-start.3 = (bf16[1,1,128,4096]{3,2,1,0:T(8,128)(2,1)S(1)}, bf16[1,1,128,4096]{3,2,1,0:T(8,128)(2,1)}, u32[]{:S(2)}) copy-start(bf16[1,1,128,4096]{3,2,1,0:T(8,128)(2,1)} %param.13) | copy-start | bytes 3145732
  19.1 23.9 %all-to-all-start.1 = ((bf16[32,4,5120]{2,1,0:T(4,128)(2,1)}), bf16[32,4,5120]{2,1,0:T(4,128)(2,1)S(1)}, u32[]{:S(2)}, u32[]{:S(2)}) async-start(bf16[32,4,5120]{2,1,0:T(4,128)(2,1)} %reshape.241), calls=%async_computation.1 | async-start | bytes 2621440 | tf_op jit(solution)/shard_map/all_to_all | solution.py:64
  23.1 13.1 %collective-permute-start.3 = (s32[128]{0:T(128)S(1)}, s32[128]{0:T(128)S(1)}, u32[]{:S(2)}, u32[]{:S(2)}) collective-permute-start(s32[128]{0:T(128)S(1)} %bitcast.89), channel_id=1, source_target_pairs={{0,1},{1,2},{2,3},{3,4},{4,5},{5,6},{6,7},{7,8},{8,9},{9,10},{10,1... | collective-permute-start | bytes 1544 | tf_op jit(solution)/shard_map/ppermute | solution.py:18
  26.9 9.3 %collective-permute-start.2 = (s32[128]{0:T(128)S(1)}, s32[128]{0:T(128)S(1)}, u32[]{:S(2)}, u32[]{:S(2)}) collective-permute-start(s32[128]{0:T(128)S(1)} %bitcast.90), channel_id=1, source_target_pairs={{0,2},{1,3},{2,4},{3,5},{4,6},{5,7},{6,8},{7,9},{8,10},{9,11},{10,... | collective-permute-start | bytes 1544 | tf_op jit(solution)/shard_map/ppermute | solution.py:18
  45.2 15.3 %collective-permute-start.1 = (bf16[128,1024]{1,0:T(8,128)(2,1)S(1)}, bf16[128,1024]{1,0:T(8,128)(2,1)S(1)}, u32[]{:S(2)}, u32[]{:S(2)}) collective-permute-start(bf16[128,1024]{1,0:T(8,128)(2,1)S(1)} %slice.30), channel_id=1, source_target_pairs={{0,1},{1,2},{2,3},{3,4},{4,5},{5,6},{6,7},{7,8},{8,9},{9,10},{10,1... | collective-permute-start | bytes 786440 | tf_op jit(solution)/shard_map/ppermute | solution.py:18
  49.0 16.8 %collective-permute-start = (bf16[128,1024]{1,0:T(8,128)(2,1)S(1)}, bf16[128,1024]{1,0:T(8,128)(2,1)S(1)}, u32[]{:S(2)}, u32[]{:S(2)}) collective-permute-start(bf16[128,1024]{1,0:T(8,128)(2,1)S(1)} %slice.30), channel_id=1, source_target_pairs={{0,2},{1,3},{2,4},{3,5},{4,6},{5,7},{6,8},{7,9},{8,10},{9,11},{10,... | collective-permute-start | bytes 786440 | tf_op jit(solution)/shard_map/ppermute | solution.py:18
  67.4 1.5 %copy-start.2 = (bf16[384,4,128,1]{0,2,3,1:T(8,128)(2,1)}, bf16[384,4,128,1]{0,2,3,1:T(8,128)(2,1)S(1)}, u32[]{:S(2)}) copy-start(bf16[384,4,128,1]{0,2,3,1:T(8,128)(2,1)S(1)} %copy.78) | copy-start | bytes 1179652
  68.9 1.4 %copy-start.4 = (bf16[1,1,128,4096]{2,3,1,0:T(8,128)(2,1)S(1)}, bf16[1,1,128,4096]{2,3,1,0:T(8,128)(2,1)}, u32[]{:S(2)}) copy-start(bf16[1,1,128,4096]{2,3,1,0:T(8,128)(2,1)} %copy.60) | copy-start | bytes 3145732
  70.3 1.6 %copy-start.5 = (bf16[384,4,128,1]{0,2,3,1:T(8,128)(2,1)S(1)}, bf16[384,4,128,1]{0,2,3,1:T(8,128)(2,1)}, u32[]{:S(2)}) copy-start(bf16[384,4,128,1]{0,2,3,1:T(8,128)(2,1)} %copy.76) | copy-start | bytes 1179652
  87.7 4.3 %copy-start.1 = (bf16[4,8,128,384]{2,3,1,0:T(8,128)(2,1)S(1)}, bf16[4,8,128,384]{2,3,1,0:T(8,128)(2,1)}, u32[]{:S(2)}) copy-start(bf16[4,8,128,384]{2,3,1,0:T(8,128)(2,1)} %fusion.2) | copy-start | bytes 9437188
  87.9 13.6 %collective-permute-start.4 = (bf16[128,1024]{1,0:T(8,128)(2,1)S(1)}, bf16[128,1024]{1,0:T(8,128)(2,1)S(1)}, u32[]{:S(2)}, u32[]{:S(2)}) collective-permute-start(bf16[128,1024]{1,0:T(8,128)(2,1)S(1)} %get-tuple-element.2), channel_id=1, source_target_pairs={{1,0},{2,1},{3,2},{4,3},{5,4},{6,5},{7,6},{8,7},{9,8},{10,9},{11,1... | collective-permute-start | bytes 786440 | tf_op jit(solution)/shard_map/ppermute | solution.py:18
  90.1 21.4 %collective-permute-start.5 = (bf16[128,1024]{1,0:T(8,128)(2,1)S(1)}, bf16[128,1024]{1,0:T(8,128)(2,1)S(1)}, u32[]{:S(2)}, u32[]{:S(2)}) collective-permute-start(bf16[128,1024]{1,0:T(8,128)(2,1)S(1)} %get-tuple-element.3), channel_id=1, source_target_pairs={{2,0},{3,1},{4,2},{5,3},{6,4},{7,5},{8,6},{9,7},{10,8},{11,9},{12,... | collective-permute-start | bytes 786440 | tf_op jit(solution)/shard_map/ppermute | solution.py:18
  113.8 24.8 %all-to-all-start.2 = ((bf16[32,4,5120]{2,1,0:T(4,128)(2,1)}), bf16[32,4,5120]{2,1,0:T(4,128)(2,1)S(1)}, u32[]{:S(2)}, u32[]{:S(2)}) async-start(bf16[32,4,5120]{2,1,0:T(4,128)(2,1)} %reshape.249), calls=%async_computation.2 | async-start | bytes 2621440 | tf_op jit(solution)/shard_map/all_to_all | solution.py:167
where the time goes:
time: 143 us; the launch traced here: 142 us
  waiting for transfers between devices  55.4 us (39%)
  starting transfers between devices  40.9 us (29%)
  matrix products  19.4 us (14%)
  local copies, waits for them, and re-layouts  17.1 us (12%)
  other arithmetic  8.53 us (6%)
    ppermute x6, waiting for transfers between devices, passed_along(): return lax.ppermute(value, axis, pairs)  27.6 us
    ppermute x6, starting transfers between devices, passed_along(): return lax.ppermute(value, axis, pairs)  24.7 us
    all_to_all x1, waiting for transfers between devices, body(): lax.all_to_all(returning.reshape(senders, capacity, width_per_row), ('enc...  16 us
    all_to_all x1, starting transfers between devices, body(): lax.all_to_all(slot_marks.reshape(senders, capacity), ('enc', 'llm'), spl...  7.32 us
    all_to_all x1, waiting for transfers between devices, body(): lax.all_to_all(outgoing.reshape(senders, capacity, width_per_row), ('enc'...  6.54 us
    all_to_all x1, waiting for transfers between devices, body(): lax.all_to_all(slot_marks.reshape(senders, capacity), ('enc', 'llm'), spl...  5.26 us
    convert_element_type x1, local copies, waits for them, and re-layouts, body(): (probs * (grad_probs - delta) * HEAD_SIZE ** (-0.5)).astype(jnp.bfloat16)  5.07 us
    all_to_all x1, starting transfers between devices, body(): lax.all_to_all(returning.reshape(senders, capacity, width_per_row), ('enc...  4.92 us
  transfers between devices with their start and end apart: 9, of which 7 were waited for; matrix products, arithmetic and copies ran while one was open for 8% of the time, Pallas kernels for 0%

commit v1 on v0

v1 whole, which is shorter than its diff:
```python
import jax
import jax.numpy as jnp
from jax import lax
from jax.experimental import pallas as pl
from jax.experimental.pallas import tpu as pltpu
from jax.sharding import PartitionSpec as P

QUERY_HEADS = 32
KEY_VALUE_HEADS = 4
HEAD_SIZE = 128
TOK = 128
IMG = 64
PATCHES = 32
N_ENC = 8
N_LLM = 4
N_SP = 16
PEERS = N_ENC * N_LLM
SLOTS = 4
COLS = (QUERY_HEADS + 2 * KEY_VALUE_HEADS) * HEAD_SIZE
GROUP = QUERY_HEADS // KEY_VALUE_HEADS
KEYS = 3 * TOK
KV = 4
PART = 1024
SCALE = HEAD_SIZE ** (-0.5)
EXP2_SCALE = SCALE * 1.4426950408889634
HIDDEN = -1e30

MESH = pl.DeviceIdType.MESH
F32 = jnp.float32
BF16 = jnp.bfloat16
I32 = jnp.int32


def iota(shape, dim):
    return lax.broadcasted_iota(I32, shape, dim)


def dot(a, b):
    return jnp.dot(a, b, preferred_element_type=F32)


def dot_t(a, b):
    return lax.dot_general(a, b, (((1,), (1,)), ((), ())), preferred_element_type=F32)


def as_column(row, size):
    eye = iota((size, size), 0) == iota((size, size), 1)
    return jnp.sum(jnp.where(eye, row, 0.0), axis=1, keepdims=True)


def one_hot(condition):
    return jnp.where(condition, 1.0, 0.0).astype(BF16)


def kernel(
    text_hbm, seg_hbm, img_hbm, count_hbm, dest_hbm, offset_hbm, cot_hbm,
    text_out, image_out,
    text, seg, img, count, dest, offset, cot,
    mark_out, mark_in, row_out, row_in, grad_out, grad_in, seg_in,
    pack, unpack, place, collect, bias, image_mask,
    kv, queries, probs_t, ds_t, far, near, own, far_in, pass_out, pass_in, kv_grad,
    text_grad, image_grad,
    load_sem, store_sem, mark_send, mark_recv, row_send, row_recv, grad_send, grad_recv,
    seg_send, seg_recv, kv_send, kv_recv, relay_send, relay_recv,
    far_send, far_recv, pass_send, pass_recv,
):
    e, l, s = lax.axis_index("enc"), lax.axis_index("llm"), lax.axis_index("sp")
    me = e * N_LLM + l
    up, up2, down, down2 = (lax.rem(s + d, N_SP) for d in (1, 2, N_SP - 1, N_SP - 2))

    loads = [
        pltpu.make_async_copy(src, dst, load_sem.at[i])
        for i, (src, dst) in enumerate(
            (
                (dest_hbm, dest), (offset_hbm, offset), (count_hbm, count), (seg_hbm, seg),
                (img_hbm, img), (text_hbm, text), (cot_hbm, cot),
            )
        )
    ]
    for load in loads:
        load.start()

    barrier = pltpu.get_barrier_semaphore()

    def peer(i):
        p = lax.rem(me + i, PEERS)
        return p, (p // N_LLM, lax.rem(p, N_LLM), s)

    def greet(i, carry):
        pl.semaphore_signal(barrier, inc=1, device_id=peer(i)[1], device_id_type=MESH)
        return carry

    lax.fori_loop(1, PEERS, greet, 0)
    for z in (down, down2, up):
        pl.semaphore_signal(barrier, inc=1, device_id=(e, l, z), device_id_type=MESH)

    for load in loads[:3]:
        load.wait()
    row_id = iota((1, IMG), 1)
    counts = jnp.where(row_id < PATCHES, count[:, 0:1], count[:, 1:2])
    live_row = lax.rem(row_id, PATCHES) < counts
    dest_row = jnp.where(live_row, dest[...], -1).astype(F32)
    dest_col = as_column(dest_row, IMG)
    offset_col = as_column(offset[...].astype(F32), IMG)
    same = (dest_col == dest_row) & (dest_row >= 0.0)
    lower = iota((IMG, IMG), 1) < iota((IMG, IMG), 0)
    higher = iota((IMG, IMG), 0) < iota((IMG, IMG), 1)
    rank_col = jnp.sum(jnp.where(same & lower, 1.0, 0.0), axis=1, keepdims=True)
    rank_row = jnp.sum(jnp.where(same & higher, 1.0, 0.0), axis=0, keepdims=True)
    slot_row = jnp.where(dest_row >= 0.0, dest_row * SLOTS + rank_row, -1.0)
    slot_col = jnp.where(dest_col >= 0.0, dest_col * SLOTS + rank_col, -1.0)
    repeat = one_hot(lax.rem(iota((IMG, 4 * IMG), 1), IMG) == iota((IMG, 4 * IMG), 0))
    slots_row = dot(jnp.broadcast_to(slot_row, (8, IMG)).astype(BF16), repeat)[0:1, :]
    tall = iota((16 * PEERS, 4 * IMG), 0)
    wide = iota((16 * PEERS, 4 * IMG), 1)
    pack[...] = one_hot(
        ((tall // 16 * SLOTS + lax.rem(tall, 4)).astype(F32) == slots_row)
        & (lax.rem(tall // 4, 4) == wide // IMG)
    )
    to_whom = one_hot(iota((PEERS, IMG), 0).astype(F32) == dest_row)
    lane = iota((IMG, TOK), 1)
    marks_mine = jnp.where(
        lane.astype(F32) == (me * SLOTS).astype(F32) + rank_col, offset_col + 1.0, 0.0
    ).astype(BF16)
    marks = dot(to_whom, marks_mine).astype(I32)
    for d in range(PEERS):
        mark_out[d] = marks[d : d + 1, :]
    mark_in[pl.ds(me, 1)] = mark_out[pl.ds(me, 1)]

    def four_tall(read):
        return jnp.concatenate(
            [jnp.concatenate([read(t, b) for b in range(4)], axis=0) for t in range(2)], axis=1
        )

    def columns(part, t, b):
        return pl.ds(pl.multiple_of(part * PART + t * 512 + b * 128, 128), 128)

    def pack_rows(part):
        packed = dot(pack[...], four_tall(lambda t, b: img[:, columns(part, t, b)])).astype(BF16)
        for t in range(2):
            row_out[part, :, t] = packed[:, t * 128 : (t + 1) * 128].reshape(PEERS, 16, 128)
        row_in[part, pl.ds(me, 1)] = row_out[part, pl.ds(me, 1)]

    def row_copy(part, i):
        p, device = peer(i)
        return pltpu.make_async_remote_copy(
            src_ref=row_out.at[part, p], dst_ref=row_in.at[part, me],
            send_sem=row_send.at[part], recv_sem=row_recv.at[part],
            device_id=device, device_id_type=MESH,
        )

    def grad_copy(part, i):
        p, device = peer(i)
        return pltpu.make_async_remote_copy(
            src_ref=grad_out.at[part, p], dst_ref=grad_in.at[part, me],
            send_sem=grad_send.at[part], recv_sem=grad_recv.at[part],
            device_id=device, device_id_type=MESH,
        )

    def mark_copy(i):
        p, device = peer(i)
        return pltpu.make_async_remote_copy(
            src_ref=mark_out.at[p], dst_ref=mark_in.at[me],
            send_sem=mark_send, recv_sem=mark_recv,
            device_id=device, device_id_type=MESH,
        )

    def start_all(copy_of):
        def one(i, carry):
            copy_of(i).start()
            return carry

        lax.fori_loop(1, PEERS, one, 0)

    def all_rows(part):
        return pltpu.make_async_remote_copy(
            src_ref=row_out.at[part, 0 : PEERS - 1], dst_ref=row_in.at[part, 0 : PEERS - 1],
            send_sem=row_send.at[part], recv_sem=row_recv.at[part],
            device_id=(e, l, up), device_id_type=MESH,
        )

    def all_grads(part):
        return pltpu.make_async_remote_copy(
            src_ref=grad_out.at[part, 0 : PEERS - 1], dst_ref=grad_in.at[part, 0 : PEERS - 1],
            send_sem=grad_send.at[part], recv_sem=grad_recv.at[part],
            device_id=(e, l, up), device_id_type=MESH,
        )

    all_marks = pltpu.make_async_remote_copy(
        src_ref=mark_out.at[0 : PEERS - 1], dst_ref=mark_in.at[0 : PEERS - 1],
        send_sem=mark_send, recv_sem=mark_recv, device_id=(e, l, up), device_id_type=MESH,
    )

    loads[4].wait()
    pack_rows(KV)
    loads[3].wait()
    pl.semaphore_wait(barrier, PEERS + 2)
    start_all(mark_copy)
    start_all(lambda i: row_copy(KV, i))
    seg_copies = [
        pltpu.make_async_remote_copy(
            src_ref=seg, dst_ref=seg_in.at[i], send_sem=seg_send.at[i], recv_sem=seg_recv.at[i],
            device_id=(e, l, z), device_id_type=MESH,
        )
        for i, z in enumerate((up, up2))
    ]
    for copy in seg_copies:
        copy.start()

    def send_queries(part, carry):
        pack_rows(part)
        start_all(lambda i: row_copy(part, i))
        return carry

    lax.fori_loop(0, KEY_VALUE_HEADS, send_queries, 0)

    slots_col = jnp.concatenate([slot_col] * 4, axis=0)
    tall = iota((4 * IMG, 16 * PEERS), 0)
    wide = iota((4 * IMG, 16 * PEERS), 1)
    unpack[...] = one_hot(
        ((wide // 16 * SLOTS + lax.rem(wide, 4)).astype(F32) == slots_col)
        & (lax.rem(wide // 4, 4) == tall // IMG)
    )

    all_marks.wait_recv()
    marks_row = jnp.sum(mark_in[...], axis=0).astype(F32)
    spread = one_hot(
        iota((TOK, 16 * PEERS), 0)
        == iota((TOK, 16 * PEERS), 1) // 16 * SLOTS + lax.rem(iota((TOK, 16 * PEERS), 1), 4)
    )
    spread_row = dot(jnp.broadcast_to(marks_row, (8, TOK)).astype(BF16), spread)[0:1, :]
    tall = iota((4 * TOK, 16 * PEERS), 0)
    wide = iota((4 * TOK, 16 * PEERS), 1)
    place[...] = one_hot(
        ((lax.rem(tall, TOK) + 1).astype(F32) == spread_row)
        & (tall // TOK == lax.rem(wide // 4, 4))
    )
    tall = iota((16 * PEERS, TOK), 0)
    wide = iota((16 * PEERS, TOK), 1)
    spread_col = jnp.sum(
        jnp.where(wide == tall // 16 * SLOTS + lax.rem(tall, 4), marks_row, 0.0),
        axis=1, keepdims=True,
    )
    tall = iota((16 * PEERS, 4 * TOK), 0)
    wide = iota((16 * PEERS, 4 * TOK), 1)
    collect[...] = one_hot(
        ((lax.rem(wide, TOK) + 1).astype(F32) == spread_col)
        & (wide // TOK == lax.rem(tall // 4, 4))
    )
    taken = jnp.sum(
        jnp.where((iota((TOK, TOK), 0) + 1).astype(F32) == marks_row, 1.0, 0.0),
        axis=1, keepdims=True,
    )
    image_mask[...] = jnp.broadcast_to(taken, (TOK, TOK))

    loads[5].wait()

    def placed(part):
        arrived = jnp.concatenate(
            [row_in[part, :, t].reshape(16 * PEERS, 128) for t in range(2)], axis=1
        )
        landed = dot(place[...], arrived)

        def block(t, b):
            rows = landed[b * 128 : (b + 1) * 128, t * 128 : (t + 1) * 128]
            text_rows = text[:, columns(part, t, b)].astype(F32)
            return jnp.where(image_mask[...] > 0.0, rows, text_rows).astype(BF16)

        return block

    def masked(rows):
        return jnp.where(image_mask[...] > 0.0, 0.0, rows).astype(BF16)

    def next_copy(g):
        return pltpu.make_async_remote_copy(
            src_ref=kv.at[g, 2 * TOK : 3 * TOK], dst_ref=kv.at[g, TOK : 2 * TOK],
            send_sem=kv_send.at[g], recv_sem=kv_recv.at[g],
            device_id=(e, l, up), device_id_type=MESH,
        )

    def relay_copy(g):
        return pltpu.make_async_remote_copy(
            src_ref=kv.at[g, TOK : 2 * TOK], dst_ref=kv.at[g, 0:TOK],
            send_sem=relay_send.at[g], recv_sem=relay_recv.at[g],
            device_id=(e, l, up), device_id_type=MESH,
        )

    def far_copy(g):
        return pltpu.make_async_remote_copy(
            src_ref=far.at[g], dst_ref=far_in.at[g],
            send_sem=far_send.at[g], recv_sem=far_recv.at[g],
            device_id=(e, l, down), device_id_type=MESH,
        )

    def pass_copy(g):
        return pltpu.make_async_remote_copy(
            src_ref=pass_out.at[g], dst_ref=pass_in.at[g],
            send_sem=pass_send.at[g], recv_sem=pass_recv.at[g],
            device_id=(e, l, down), device_id_type=MESH,
        )

    all_rows(KV).wait_recv()
    block = placed(KV)
    for g in range(KEY_VALUE_HEADS):
        for t in range(2):
            kv[g, 2 * TOK : 3 * TOK, t * 128 : (t + 1) * 128] = block(t, g)
        next_copy(g).start()

    for copy in seg_copies:
        copy.wait_recv()
    seg_row = seg[...].astype(F32)
    seg_near = jnp.where(s >= 1, as_column(seg_in[0].astype(F32), TOK), -1.0)
    seg_far = jnp.where(s >= 2, as_column(seg_in[1].astype(F32), TOK), -1.0)
    seg_own = as_column(seg_row, TOK)
    for i, column in enumerate((seg_far, seg_near, seg_own)):
        visible = column == seg_row
        if i == 2:
            visible = visible & (iota((TOK, TOK), 0) <= iota((TOK, TOK), 1))
        hidden = jnp.where(visible, 0.0, HIDDEN)
        for h in range(2):
            bias[i * TOK : (i + 1) * TOK, h * 128 : (h + 1) * 128] = hidden

    def relay(g):
        next_copy(g).wait_recv()
        relay_copy(g).start()

    def chain(g):
        far_copy(g).wait_recv()
        pass_out[g] = (near[g] + far_in[g].astype(F32)).astype(BF16)
        pass_copy(g).start()

    def finish(g):
        pass_copy(g).wait_recv()
        total = (own[g] + pass_in[g].astype(F32)).astype(BF16)
        kv_grad[g] = total
        for t in range(2):
            text_grad[:, columns(KV, t, g)] = masked(
                total[:, t * 128 : (t + 1) * 128].astype(F32)
            )

    def return_rows(part, read):
        gathered = dot(collect[...], four_tall(read)).astype(BF16)
        for t in range(2):
            grad_out[part, :, t] = gathered[:, t * 128 : (t + 1) * 128].reshape(PEERS, 16, 128)
        grad_in[part, pl.ds(me, 1)] = grad_out[part, pl.ds(me, 1)]
        start_all(lambda i: grad_copy(part, i))

    def part_columns(part):
        return pl.ds(pl.multiple_of(part * PART, PART), PART)

    def text_store(part):
        return pltpu.make_async_copy(
            text_grad.at[:, part_columns(part)], text_out.at[:, part_columns(part)],
            store_sem.at[0, part],
        )

    def image_store(part):
        return pltpu.make_async_copy(
            image_grad.at[:, part_columns(part)], image_out.at[:, part_columns(part)],
            store_sem.at[1, part],
        )

    eye = one_hot(iota((128, 128), 0) == iota((128, 128), 1))
    loads[6].wait()
    relay(0)
    relay(1)

    def group(g, carry):
        all_rows(g).wait_recv()
        block = placed(g)
        for t in range(2):
            for b in range(4):
                h = t * 4 + b
                queries[h * 128 : (h + 1) * 128, :] = block(t, b)

        @pl.when(g < 2)
        def _():
            relay(g + 2)

        relay_copy(g).wait_recv()
        keys = kv[g, :, 0:128]
        values = kv[g, :, 128:256]
        keys_t = dot_t(eye, keys).astype(BF16)
        cots = [
            cot[:, pl.ds(pl.multiple_of(g * PART + h * 128, 128), 128)] for h in range(GROUP)
        ]
        grads = []
        for pair in range(GROUP // 2):
            q = queries[pair * 256 : (pair + 1) * 256, :]
            d_out = jnp.concatenate(cots[2 * pair : 2 * pair + 2], axis=0)
            logits = dot_t(keys, q) + bias[...]
            top = jnp.max(logits, axis=0, keepdims=True)
            raised = jnp.exp2((logits - top) * EXP2_SCALE)
            inverse = 1.0 / jnp.sum(raised, axis=0, keepdims=True)
            grad_probs = dot_t(values, d_out)
            delta = jnp.sum(raised * grad_probs, axis=0, keepdims=True) * inverse
            probs_t[:, pair * 256 : (pair + 1) * 256] = (raised * inverse).astype(BF16)
            ds = (raised * ((grad_probs - delta) * (inverse * SCALE))).astype(BF16)
            ds_t[:, pair * 256 : (pair + 1) * 256] = ds
            grad_t = dot(keys_t, ds).astype(BF16)
            for i in range(2):
                grads.append(dot_t(eye, grad_t[:, i * 128 : (i + 1) * 128]).astype(BF16))
        key_grad = dot(ds_t[...], queries[...])
        value_grad = dot(probs_t[...], jnp.concatenate(cots, axis=0))
        for t, grad in enumerate((key_grad, value_grad)):
            half = slice(t * 128, (t + 1) * 128)
            far[g, :, half] = grad[0:TOK].astype(BF16)
            near[g, :, half] = grad[TOK : 2 * TOK]
            own[g, :, half] = grad[2 * TOK : 3 * TOK]
        far_copy(g).start()
        return_rows(g, lambda t, b: grads[t * 4 + b])
        for t in range(2):
            for b in range(4):
                text_grad[:, columns(g, t, b)] = masked(grads[t * 4 + b].astype(F32))
        text_store(g).start()

        @pl.when(g >= 1)
        def _():
            chain(g - 1)

        @pl.when(g >= 2)
        def _():
            finish(g - 2)

        return carry

    lax.fori_loop(0, KEY_VALUE_HEADS, group, 0)
    chain(3)
    finish(2)
    finish(3)
    return_rows(KV, lambda t, b: kv_grad[b, :, t * 128 : (t + 1) * 128])
    text_store(KV).start()

    def take_back(part, carry):
        all_grads(part).wait_recv()
        returned = jnp.concatenate(
            [grad_in[part, :, t].reshape(16 * PEERS, 128) for t in range(2)], axis=1
        )
        back = dot(unpack[...], returned).astype(BF16)
        for t in range(2):
            for b in range(4):
                image_grad[:, columns(part, t, b)] = back[
                    b * IMG : (b + 1) * IMG, t * 128 : (t + 1) * 128
                ]
        image_store(part).start()
        return carry

    lax.fori_loop(0, KV + 1, take_back, 0)

    all_marks.wait_send()
    for copy in seg_copies:
        copy.wait_send()

    def drain(part, carry):
        all_rows(part).wait_send()
        all_grads(part).wait_send()
        text_store(part).wait()
        image_store(part).wait()
        return carry

    lax.fori_loop(0, KV + 1, drain, 0)

    def drain_halo(g, carry):
        for copy in (next_copy, relay_copy, far_copy, pass_copy):
            copy(g).wait_send()
        return carry

    lax.fori_loop(0, KEY_VALUE_HEADS, drain_halo, 0)


def body(text_qkv, segments, image_qkv, patch_counts, image_dest, image_offset, output_cotangent):
    hbm = pl.BlockSpec(memory_space=pl.ANY)
    dma = pltpu.SemaphoreType.DMA
    q_cols = QUERY_HEADS * HEAD_SIZE
    tiles = (KV + 1, PEERS, 2, 16, 128)
    halo = (KEY_VALUE_HEADS, TOK, 256)
    text_grad, image_grad = pl.pallas_call(
        kernel,
        name="slab",
        out_shape=(
            jax.ShapeDtypeStruct((TOK, COLS), BF16),
            jax.ShapeDtypeStruct((IMG, COLS), BF16),
        ),
        in_specs=[hbm] * 7,
        out_specs=(hbm, hbm),
        scratch_shapes=[
            pltpu.VMEM((TOK, COLS), BF16),
            pltpu.VMEM((1, TOK), I32),
            pltpu.VMEM((IMG, COLS), BF16),
            pltpu.VMEM((1, 2), I32),
            pltpu.VMEM((1, IMG), I32),
            pltpu.VMEM((1, IMG), I32),
            pltpu.VMEM((TOK, q_cols), BF16),
            pltpu.VMEM((PEERS, 1, TOK), I32),
            pltpu.VMEM((PEERS, 1, TOK), I32),
            pltpu.VMEM(tiles, BF16),
            pltpu.VMEM(tiles, BF16),
            pltpu.VMEM(tiles, BF16),
            pltpu.VMEM(tiles, BF16),
            pltpu.VMEM((2, 1, TOK), I32),
            pltpu.VMEM((16 * PEERS, 4 * IMG), BF16),
            pltpu.VMEM((4 * IMG, 16 * PEERS), BF16),
            pltpu.VMEM((4 * TOK, 16 * PEERS), BF16),
            pltpu.VMEM((16 * PEERS, 4 * TOK), BF16),
            pltpu.VMEM((KEYS, 256), F32),
            pltpu.VMEM((TOK, 128), F32),
            pltpu.VMEM((KEY_VALUE_HEADS, KEYS, 256), BF16),
            pltpu.VMEM((GROUP * TOK, 128), BF16),
            pltpu.VMEM((KEYS, GROUP * TOK), BF16),
            pltpu.VMEM((KEYS, GROUP * TOK), BF16),
            pltpu.VMEM(halo, BF16),
            pltpu.VMEM(halo, F32),
            pltpu.VMEM(halo, F32),
            pltpu.VMEM(halo, BF16),
            pltpu.VMEM(halo, BF16),
            pltpu.VMEM(halo, BF16),
            pltpu.VMEM(halo, BF16),
            pltpu.VMEM((TOK, COLS), BF16),
            pltpu.VMEM((IMG, COLS), BF16),
            dma((7,)),
            dma((2, KV + 1)),
            dma, dma,
            dma((KV + 1,)), dma((KV + 1,)), dma((KV + 1,)), dma((KV + 1,)),
            dma((2,)), dma((2,)),
            dma((4,)), dma((4,)), dma((4,)), dma((4,)),
            dma((4,)), dma((4,)), dma((4,)), dma((4,)),
        ],
        compiler_params=pltpu.CompilerParams(
            collective_id=0, has_side_effects=True, vmem_limit_bytes=56 << 20
        ),
        cost_estimate=pl.CostEstimate(
            flops=4 << 30, bytes_accessed=5 << 20, transcendentals=2 << 20
        ),
    )(
        text_qkv[0, 0], segments[0], image_qkv[0, 0, 0], patch_counts[0, 0],
        image_dest[0, 0], image_offset[0, 0], output_cotangent[0, 0],
    )
    return text_grad[None, None], image_grad[None, None, None]


def solution(mesh):
    rows = P("enc", "llm", "sp", None)
    deep = P("enc", "llm", "sp", None, None)
    return jax.shard_map(
        body, mesh=mesh,
        in_specs=(rows, P("enc", "llm", "sp"), deep, rows, rows, rows, rows),
        out_specs=(rows, deep), check_vma=False,
    )
```

time: 143 us -> 64.8 us (0.45)
  the two profiles are of different devices: /device:TPU:64 before, /device:TPU:1 now
where the time goes in v1:
time: 64.8 us; the launch traced here: 64.6 us
  Pallas kernels  60.6 us (94%)
  local copies, waits for them, and re-layouts  3.36 us (5%)
  between operations  0.65 us (1%)
    pallas_call x1, Pallas kernels, body(): pl.pallas_call(kernel, name='slab', out_shape=(jax.ShapeDtypeStruct((TOK,...  60.6 us
    unnamed x4, local copies, waits for them, and re-layouts  3.36 us

profile of v1, /device:TPU:1, one launch (start us, length us, event | category | flops | bytes accessed | tf_op | source)
XLA Modules:
  0.0 64.6 jit_solution(4065863991943393283)
XLA Ops:
  0.6 60.6 %slab.1 = (bf16[128,5120]{1,0:T(8,128)(2,1)}, bf16[64,5120]{1,0:T(8,128)(2,1)}) custom-call(bf16[128,5120]{1,0:T(8,128)(2,1)} %bitcast.11, s32[1,128]{1,0:T(1,128)} %bitcast.14, bf16[64,5120]{1,0:T(8,128)(2,1)} %bitcast.13, s32[1,2]{1,0:T(1,128)} %bitcast.15, s32[1,64]{1,0:T(1,128)} %bitcast.16, s32[1,64]{1,0:T(1,128)} %bitcast.17, bf16[128,4096]{1,0:T(8,128)(2,1)} %bitcast.12), custom_call_target="tpu_custom_call" | custom-call | flops 4294967296 | bytes 5242880 | tf_op jit(solution)/shard_map/slab/pallas_call | solution.py:477
  61.2 0.0 copy-start
  61.2 2.5 %copy.11 = bf16[1,1,128,5120]{3,2,1,0:T(8,128)(2,1)} copy(bf16[1,1,128,5120]{3,2,1,0:T(8,128)(2,1)} %bitcast.9) | data formatting | bytes 2621440
  63.8 0.0 copy-done
  63.8 0.8 %copy.12 = bf16[1,1,1,64,5120]{4,3,2,1,0:T(8,128)(2,1)} copy(bf16[1,1,1,64,5120]{4,3,2,1,0:T(8,128)(2,1)S(1)} %bitcast.10) | data formatting | bytes 1310720
Async XLA Ops:
  61.2 2.5 %copy-start = (bf16[64,5120]{1,0:T(8,128)(2,1)S(1)}, bf16[64,5120]{1,0:T(8,128)(2,1)}, u32[]{:S(2)}) copy-start(bf16[64,5120]{1,0:T(8,128)(2,1)} %get-tuple-element.5) | copy-start | bytes 1966084

commit v2 on v1

v2 whole, which is shorter than its diff:
```python
import jax
import jax.numpy as jnp
from jax import lax
from jax.experimental import pallas as pl
from jax.experimental.pallas import tpu as pltpu
from jax.sharding import PartitionSpec as P

QUERY_HEADS = 32
KEY_VALUE_HEADS = 4
HEAD_SIZE = 128
TOK = 128
IMG = 64
PATCHES = 32
N_ENC = 8
N_LLM = 4
N_SP = 16
PEERS = N_ENC * N_LLM
SLOTS = 4
COLS = (QUERY_HEADS + 2 * KEY_VALUE_HEADS) * HEAD_SIZE
GROUP = QUERY_HEADS // KEY_VALUE_HEADS
KEYS = 3 * TOK
PARTS = 6
PART = 1024
SCALE = HEAD_SIZE ** (-0.5)
EXP2_SCALE = SCALE * 1.4426950408889634
HIDDEN = -1e30

MESH = pl.DeviceIdType.MESH
F32 = jnp.float32
BF16 = jnp.bfloat16
I32 = jnp.int32


def iota(shape, dim):
    return lax.broadcasted_iota(I32, shape, dim)


def dot(a, b):
    return jnp.dot(a, b, preferred_element_type=F32)


def dot_t(a, b):
    return lax.dot_general(a, b, (((1,), (1,)), ((), ())), preferred_element_type=F32)


def as_column(row, size):
    eye = iota((size, size), 0) == iota((size, size), 1)
    return jnp.sum(jnp.where(eye, row, 0.0), axis=1, keepdims=True)


def one_hot(condition):
    return jnp.where(condition, 1.0, 0.0).astype(BF16)


def kernel(
    text_hbm, seg_hbm, img_hbm, count_hbm, dest_hbm, offset_hbm, cot_hbm,
    text_grad, image_grad,
    text, seg, img, count, dest, offset, cot,
    mark_out, mark_in, row_out, row_in, grad_out, grad_in,
    kv_rows_out, kv_rows_in, kv_grads_out, kv_grads_in, seg_in,
    pack, unpack, place, collect, bias, causal, image_mask,
    kv, queries, probs_t, ds_t, far, near, own, far_in, pass_out, pass_in, kv_grad,
    load_sem, mark_send, mark_recv, row_send, row_recv, grad_send, grad_recv,
    seg_send, seg_recv, kv_send, kv_recv, relay_send, relay_recv,
    far_send, far_recv, pass_send, pass_recv,
):
    e, l, s = lax.axis_index("enc"), lax.axis_index("llm"), lax.axis_index("sp")
    me = e * N_LLM + l
    up, up2, down, down2 = (lax.rem(s + d, N_SP) for d in (1, 2, N_SP - 1, N_SP - 2))

    loads = [
        pltpu.make_async_copy(src, dst, load_sem.at[i])
        for i, (src, dst) in enumerate(
            (
                (dest_hbm, dest), (offset_hbm, offset), (count_hbm, count), (seg_hbm, seg),
                (img_hbm, img), (text_hbm, text), (cot_hbm, cot),
            )
        )
    ]
    for load in loads:
        load.start()

    barrier = pltpu.get_barrier_semaphore()

    def peer(i):
        p = lax.rem(me + i, PEERS)
        return p, (p // N_LLM, lax.rem(p, N_LLM), s)

    def greet(i, carry):
        pl.semaphore_signal(barrier, inc=1, device_id=peer(i)[1], device_id_type=MESH)
        return carry

    lax.fori_loop(1, PEERS, greet, 0)
    for z in (down, down2, up):
        pl.semaphore_signal(barrier, inc=1, device_id=(e, l, z), device_id_type=MESH)

    for load in loads[:3]:
        load.wait()
    row_id = iota((1, IMG), 1)
    counts = jnp.where(row_id < PATCHES, count[:, 0:1], count[:, 1:2])
    live_row = lax.rem(row_id, PATCHES) < counts
    dest_row = jnp.where(live_row, dest[...], -1).astype(F32)
    dest_col = as_column(dest_row, IMG)
    offset_col = as_column(offset[...].astype(F32), IMG)
    same = (dest_col == dest_row) & (dest_row >= 0.0)
    lower = iota((IMG, IMG), 1) < iota((IMG, IMG), 0)
    higher = iota((IMG, IMG), 0) < iota((IMG, IMG), 1)
    rank_col = jnp.sum(jnp.where(same & lower, 1.0, 0.0), axis=1, keepdims=True)
    rank_row = jnp.sum(jnp.where(same & higher, 1.0, 0.0), axis=0, keepdims=True)
    slot_row = jnp.where(dest_row >= 0.0, dest_row * SLOTS + rank_row, -1.0)
    slot_col = jnp.where(dest_col >= 0.0, dest_col * SLOTS + rank_col, -1.0)
    repeat = one_hot(lax.rem(iota((IMG, 4 * IMG), 1), IMG) == iota((IMG, 4 * IMG), 0))
    slots_row = dot(jnp.broadcast_to(slot_row, (8, IMG)).astype(BF16), repeat)[0:1, :]
    codes_row = slots_row.astype(I32) * 4 + iota((1, 4 * IMG), 1) // IMG
    pack[...] = one_hot(iota((16 * PEERS, 4 * IMG), 0) == codes_row)
    to_whom = one_hot(iota((PEERS, IMG), 0).astype(F32) == dest_row)
    lane = iota((IMG, TOK), 1)
    marks_mine = jnp.where(
        lane.astype(F32) == (me * SLOTS).astype(F32) + rank_col, offset_col + 1.0, 0.0
    ).astype(BF16)
    marks = dot(to_whom, marks_mine).astype(I32)
    for d in range(PEERS):
        mark_out[d] = marks[d : d + 1, :]
    mark_in[pl.ds(me, 1)] = mark_out[pl.ds(me, 1)]

    def four_tall(read, tiles):
        return jnp.concatenate(
            [jnp.concatenate([read(t, b) for b in range(4)], axis=0) for t in tiles], axis=1
        )

    def q_columns(g, t, b):
        return pl.ds(pl.multiple_of(g * PART + t * 512 + b * 128, 128), 128)

    def kv_columns(g, t):
        return slice(4096 + t * 512 + g * 128, 4096 + t * 512 + g * 128 + 128)

    def pack_queries(g):
        packed = dot(pack[...], four_tall(lambda t, b: img[:, q_columns(g, t, b)], (0, 1)))
        packed = packed.astype(BF16)
        for t in range(2):
            row_out[g, :, t] = packed[:, t * 128 : (t + 1) * 128].reshape(PEERS, 16, 128)
        row_in[g, pl.ds(me, 1)] = row_out[g, pl.ds(me, 1)]

    def pack_kv():
        packed = dot(
            pack[...],
            four_tall(lambda t, b: img[:, kv_columns(2 * t + b // 2, b % 2)], (0, 1)),
        ).astype(BF16)
        for t in range(2):
            kv_rows_out[t] = packed[:, t * 128 : (t + 1) * 128].reshape(PEERS, 16, 128)
            kv_rows_in[t, pl.ds(me, 1)] = kv_rows_out[t, pl.ds(me, 1)]

    def scatter(source, target, send_sem, recv_sem):
        def copy_of(i):
            p, device = peer(i)
            return pltpu.make_async_remote_copy(
                src_ref=source.at[p], dst_ref=target.at[me], send_sem=send_sem,
                recv_sem=recv_sem, device_id=device, device_id_type=MESH,
            )

        def three(n, carry):
            for i in range(3):
                copy_of(n * 3 + i + 1).start()
            return carry

        lax.fori_loop(0, (PEERS - 1) // 3, three, 0)
        copy_of(PEERS - 1).start()

    def whole(source, target, send_sem, recv_sem):
        return pltpu.make_async_remote_copy(
            src_ref=source.at[0 : PEERS - 1], dst_ref=target.at[0 : PEERS - 1],
            send_sem=send_sem, recv_sem=recv_sem, device_id=(e, l, up), device_id_type=MESH,
        )

    def rows_of(g):
        return row_out.at[g], row_in.at[g], row_send.at[g], row_recv.at[g]

    def kv_rows_of(t):
        return kv_rows_out.at[t], kv_rows_in.at[t], row_send.at[4 + t], row_recv.at[4 + t]

    def grads_of(g):
        return grad_out.at[g], grad_in.at[g], grad_send.at[g], grad_recv.at[g]

    def kv_grads_of(t):
        return kv_grads_out.at[t], kv_grads_in.at[t], grad_send.at[4 + t], grad_recv.at[4 + t]

    marks_of = (mark_out, mark_in, mark_send, mark_recv)

    loads[4].wait()
    pack_kv()
    loads[3].wait()
    pl.semaphore_wait(barrier, PEERS + 2)
    scatter(*marks_of)
    scatter(*kv_rows_of(0))
    scatter(*kv_rows_of(1))
    seg_copies = [
        pltpu.make_async_remote_copy(
            src_ref=seg, dst_ref=seg_in.at[i], send_sem=seg_send.at[i], recv_sem=seg_recv.at[i],
            device_id=(e, l, z), device_id_type=MESH,
        )
        for i, z in enumerate((up, up2))
    ]
    for copy in seg_copies:
        copy.start()

    def send_queries(g, carry):
        pack_queries(g)
        scatter(*rows_of(g))
        return carry

    lax.fori_loop(0, KEY_VALUE_HEADS, send_queries, 0)

    slots_col = jnp.concatenate([slot_col] * 4, axis=0)
    codes_col = slots_col.astype(I32) * 4 + iota((4 * IMG, 1), 0) // IMG
    unpack[...] = one_hot(codes_col == iota((4 * IMG, 16 * PEERS), 1))

    for copy in seg_copies:
        copy.wait_recv()
    seg_row = seg[...].astype(F32)
    seg_near = jnp.where(s >= 1, as_column(seg_in[0].astype(F32), TOK), -1.0)
    seg_far = jnp.where(s >= 2, as_column(seg_in[1].astype(F32), TOK), -1.0)
    seg_own = as_column(seg_row, TOK)
    earlier = iota((TOK, TOK), 0) <= iota((TOK, TOK), 1)
    near_bias = jnp.where(seg_near == seg_row, 0.0, HIDDEN)
    rest_bias = jnp.where(jnp.where(earlier, seg_own, seg_far) == seg_row, 0.0, HIDDEN)
    for h in range(2):
        half = slice(h * 128, (h + 1) * 128)
        bias[0:TOK, half] = rest_bias
        bias[TOK : 2 * TOK, half] = near_bias
        causal[:, half] = jnp.where(earlier, 1.0, 0.0)

    whole(*marks_of).wait_recv()
    marks_row = jnp.sum(mark_in[...], axis=0).astype(F32)
    spread = one_hot(iota((TOK, 16 * PEERS), 0) == iota((TOK, 16 * PEERS), 1) // 4)
    spread_row = dot(jnp.broadcast_to(marks_row, (8, TOK)).astype(BF16), spread)[0:1, :]
    codes_row = spread_row.astype(I32) + lax.rem(iota((1, 16 * PEERS), 1), 4) * 256
    tall = iota((4 * TOK, 1), 0)
    codes_col = lax.rem(tall, TOK) + 1 + tall // TOK * 256
    place[...] = one_hot(codes_col == codes_row)
    taken = jnp.sum(
        jnp.where((iota((TOK, TOK), 0) + 1).astype(F32) == marks_row, 1.0, 0.0),
        axis=1, keepdims=True,
    )
    image_mask[...] = jnp.broadcast_to(taken, (TOK, TOK))
    loads[5].wait()

    def mixed(landed, text_rows):
        return jnp.where(image_mask[...] > 0.0, landed, text_rows.astype(F32)).astype(BF16)

    def masked(rows):
        return jnp.where(image_mask[...] > 0.0, 0.0, rows).astype(BF16)

    def next_copy(g):
        return pltpu.make_async_remote_copy(
            src_ref=kv.at[g, 2 * TOK : 3 * TOK], dst_ref=kv.at[g, TOK : 2 * TOK],
            send_sem=kv_send.at[g], recv_sem=kv_recv.at[g],
            device_id=(e, l, up), device_id_type=MESH,
        )

    def relay_copy(g):
        return pltpu.make_async_remote_copy(
            src_ref=kv.at[g, TOK : 2 * TOK], dst_ref=kv.at[g, 0:TOK],
            send_sem=relay_send.at[g], recv_sem=relay_recv.at[g],
            device_id=(e, l, up), device_id_type=MESH,
        )

    def far_copy(g):
        return pltpu.make_async_remote_copy(
            src_ref=far.at[g], dst_ref=far_in.at[g],
            send_sem=far_send.at[g], recv_sem=far_recv.at[g],
            device_id=(e, l, down), device_id_type=MESH,
        )

    def pass_copy(g):
        return pltpu.make_async_remote_copy(
            src_ref=pass_out.at[g], dst_ref=pass_in.at[g],
            send_sem=pass_send.at[g], recv_sem=pass_recv.at[g],
            device_id=(e, l, down), device_id_type=MESH,
        )

    def relay(g):
        next_copy(g).wait_recv()
        relay_copy(g).start()

    def place_kv(t):
        whole(*kv_rows_of(t)).wait_recv()
        landed = dot(place[...], kv_rows_in[t].reshape(16 * PEERS, 128))
        for b in range(4):
            g, half = 2 * t + b // 2, b % 2
            kv[g, 2 * TOK : 3 * TOK, half * 128 : (half + 1) * 128] = mixed(
                landed[b * 128 : (b + 1) * 128], text[:, kv_columns(g, half)]
            )

    place_kv(0)
    next_copy(0).start()
    next_copy(1).start()
    place_kv(1)

    tall = iota((16 * PEERS, TOK), 0)
    spread_col = jnp.sum(
        jnp.where(iota((16 * PEERS, TOK), 1) == tall // 4, marks_row, 0.0),
        axis=1, keepdims=True,
    )
    codes_col = spread_col.astype(I32) + lax.rem(iota((16 * PEERS, 1), 0), 4) * 256
    wide = iota((1, 4 * TOK), 1)
    collect[...] = one_hot(codes_col == lax.rem(wide, TOK) + 1 + wide // TOK * 256)

    relay(0)
    next_copy(2).start()
    relay(1)
    next_copy(3).start()

    def chain(g):
        far_copy(g).wait_recv()
        pass_out[g] = (near[g] + far_in[g].astype(F32)).astype(BF16)
        pass_copy(g).start()

    def finish(g):
        pass_copy(g).wait_recv()
        kv_grad[g] = (own[g] + pass_in[g].astype(F32)).astype(BF16)

    loads[6].wait()

    def group(g, carry):
        whole(*rows_of(g)).wait_recv()
        arrived = jnp.concatenate(
            [row_in[g, :, t].reshape(16 * PEERS, 128) for t in range(2)], axis=1
        )
        landed = dot(place[...], arrived)
        for t in range(2):
            for b in range(4):
                h = t * 4 + b
                queries[h * 128 : (h + 1) * 128, :] = mixed(
                    landed[b * 128 : (b + 1) * 128, t * 128 : (t + 1) * 128],
                    text[:, q_columns(g, t, b)],
                )

        relay_copy(g).wait_recv()
        keys = kv[g, :, 0:128]
        values = kv[g, :, 128:256]
        cots = [
            cot[:, pl.ds(pl.multiple_of(g * PART + h * 128, 128), 128)] for h in range(GROUP)
        ]
        is_own = causal[...] > 0.0
        own_part = causal[...].astype(BF16)
        far_part = (1.0 - causal[...]).astype(BF16)

        def two_blocks(products):
            rest = jnp.where(is_own, products[2 * TOK :], products[0:TOK])
            return jnp.concatenate([rest, products[TOK : 2 * TOK]], axis=0)

        for pair in range(GROUP // 2):
            both = slice(pair * 256, (pair + 1) * 256)
            d_out = jnp.concatenate(cots[2 * pair : 2 * pair + 2], axis=0)
            logits = two_blocks(dot_t(keys, queries[both, :])) + bias[...]
            grad_probs = two_blocks(dot_t(values, d_out))
            top = jnp.max(logits, axis=0, keepdims=True)
            raised = jnp.exp2((logits - top) * EXP2_SCALE)
            inverse = 1.0 / jnp.sum(raised, axis=0, keepdims=True)
            delta = jnp.sum(raised * grad_probs, axis=0, keepdims=True) * inverse
            probs = (raised * inverse).astype(BF16)
            ds = (raised * ((grad_probs - delta) * (inverse * SCALE))).astype(BF16)
            for target, value in ((probs_t, probs), (ds_t, ds)):
                target[0:TOK, both] = value[0:TOK] * far_part
                target[TOK : 2 * TOK, both] = value[TOK : 2 * TOK]
                target[2 * TOK : 3 * TOK, both] = value[0:TOK] * own_part
        key_grad = dot(ds_t[...], queries[...])
        value_grad = dot(probs_t[...], jnp.concatenate(cots, axis=0))
        for t, grad in enumerate((key_grad, value_grad)):
            half = slice(t * 128, (t + 1) * 128)
            far[g, :, half] = grad[0:TOK].astype(BF16)
            near[g, :, half] = grad[TOK : 2 * TOK]
            own[g, :, half] = grad[2 * TOK : 3 * TOK]
        far_copy(g).start()

        @pl.when(g < 2)
        def _():
            relay(g + 2)

        grads_t = dot(keys.T, ds_t[...]).astype(BF16)
        grads = [grads_t[:, h * 128 : (h + 1) * 128].T for h in range(GROUP)]
        gathered = dot(collect[...], four_tall(lambda t, b: grads[t * 4 + b], (0, 1)))
        gathered = gathered.astype(BF16)
        for t in range(2):
            grad_out[g, :, t] = gathered[:, t * 128 : (t + 1) * 128].reshape(PEERS, 16, 128)
        grad_in[g, pl.ds(me, 1)] = grad_out[g, pl.ds(me, 1)]
        scatter(*grads_of(g))

        @pl.when(g >= 1)
        def _():
            chain(g - 1)

        for t in range(2):
            for b in range(4):
                text_grad[:, q_columns(g, t, b)] = masked(grads[t * 4 + b].astype(F32))

        @pl.when(g >= 2)
        def _():
            finish(g - 2)

        return carry

    lax.fori_loop(0, KEY_VALUE_HEADS, group, 0)

    def return_kv(t):
        rows = four_tall(
            lambda _, b: kv_grad[2 * t + b // 2, :, b % 2 * 128 : (b % 2 + 1) * 128], (0,)
        )
        kv_grads_out[t] = dot(collect[...], rows).astype(BF16).reshape(PEERS, 16, 128)
        kv_grads_in[t, pl.ds(me, 1)] = kv_grads_out[t, pl.ds(me, 1)]
        scatter(*kv_grads_of(t))

    def take_back(g, carry):
        whole(*grads_of(g)).wait_recv()
        returned = jnp.concatenate(
            [grad_in[g, :, t].reshape(16 * PEERS, 128) for t in range(2)], axis=1
        )
        back = dot(unpack[...], returned).astype(BF16)
        for t in range(2):
            for b in range(4):
                image_grad[:, q_columns(g, t, b)] = back[
                    b * IMG : (b + 1) * IMG, t * 128 : (t + 1) * 128
                ]
        return carry

    return_kv(0)
    chain(3)
    finish(2)
    take_back(0, 0)
    finish(3)
    return_kv(1)
    for g in range(KEY_VALUE_HEADS):
        for t in range(2):
            text_grad[:, kv_columns(g, t)] = masked(
                kv_grad[g, :, t * 128 : (t + 1) * 128].astype(F32)
            )
    lax.fori_loop(1, KEY_VALUE_HEADS, take_back, 0)

    whole(*marks_of).wait_send()
    for copy in seg_copies:
        copy.wait_send()

    def drain(g, carry):
        whole(*rows_of(g)).wait_send()
        whole(*grads_of(g)).wait_send()
        for copy in (next_copy, relay_copy, far_copy, pass_copy):
            copy(g).wait_send()
        return carry

    lax.fori_loop(0, KEY_VALUE_HEADS, drain, 0)
    for t in range(2):
        whole(*kv_rows_of(t)).wait_send()
        whole(*kv_grads_of(t)).wait()
        back = dot(unpack[...], kv_grads_in[t].reshape(16 * PEERS, 128)).astype(BF16)
        for b in range(4):
            image_grad[:, kv_columns(2 * t + b // 2, b % 2)] = back[b * IMG : (b + 1) * IMG]


def write_out(text_grad, image_grad, text_out, image_out, sem):
    copies = [
        pltpu.make_async_copy(text_grad, text_out, sem.at[0]),
        pltpu.make_async_copy(image_grad, image_out, sem.at[1]),
    ]
    for copy in copies:
        copy.start()
    for copy in copies:
        copy.wait()


def body(text_qkv, segments, image_qkv, patch_counts, image_dest, image_offset, output_cotangent):
    hbm = pl.BlockSpec(memory_space=pl.ANY)
    dma = pltpu.SemaphoreType.DMA
    q_cols = QUERY_HEADS * HEAD_SIZE
    tiles = (KEY_VALUE_HEADS, PEERS, 2, 16, 128)
    kv_tiles = (2, PEERS, 16, 128)
    vmem = pl.BlockSpec(memory_space=pltpu.VMEM)
    halo = (KEY_VALUE_HEADS, TOK, 256)
    text_grad, image_grad = pl.pallas_call(
        kernel,
        name="slab",
        out_shape=(pltpu.VMEM((TOK, COLS), BF16), pltpu.VMEM((IMG, COLS), BF16)),
        in_specs=[pl.BlockSpec(memory_space=pltpu.HBM)] * 7,
        out_specs=(vmem, vmem),
        scratch_shapes=[
            pltpu.VMEM((TOK, COLS), BF16),
            pltpu.VMEM((1, TOK), I32),
            pltpu.VMEM((IMG, COLS), BF16),
            pltpu.VMEM((1, 2), I32),
            pltpu.VMEM((1, IMG), I32),
            pltpu.VMEM((1, IMG), I32),
            pltpu.VMEM((TOK, q_cols), BF16),
            pltpu.VMEM((PEERS, 1, TOK), I32),
            pltpu.VMEM((PEERS, 1, TOK), I32),
            pltpu.VMEM(tiles, BF16),
            pltpu.VMEM(tiles, BF16),
            pltpu.VMEM(tiles, BF16),
            pltpu.VMEM(tiles, BF16),
            pltpu.VMEM(kv_tiles, BF16),
            pltpu.VMEM(kv_tiles, BF16),
            pltpu.VMEM(kv_tiles, BF16),
            pltpu.VMEM(kv_tiles, BF16),
            pltpu.VMEM((2, 1, TOK), I32),
            pltpu.VMEM((16 * PEERS, 4 * IMG), BF16),
            pltpu.VMEM((4 * IMG, 16 * PEERS), BF16),
            pltpu.VMEM((4 * TOK, 16 * PEERS), BF16),
            pltpu.VMEM((16 * PEERS, 4 * TOK), BF16),
            pltpu.VMEM((2 * TOK, 256), F32),
            pltpu.VMEM((TOK, 256), F32),
            pltpu.VMEM((TOK, 128), F32),
            pltpu.VMEM((KEY_VALUE_HEADS, KEYS, 256), BF16),
            pltpu.VMEM((GROUP * TOK, 128), BF16),
            pltpu.VMEM((KEYS, GROUP * TOK), BF16),
            pltpu.VMEM((KEYS, GROUP * TOK), BF16),
            pltpu.VMEM(halo, BF16),
            pltpu.VMEM(halo, F32),
            pltpu.VMEM(halo, F32),
            pltpu.VMEM(halo, BF16),
            pltpu.VMEM(halo, BF16),
            pltpu.VMEM(halo, BF16),
            pltpu.VMEM(halo, BF16),
            dma((7,)),
            dma, dma,
            dma((PARTS,)), dma((PARTS,)), dma((PARTS,)), dma((PARTS,)),
            dma((2,)), dma((2,)),
            dma((4,)), dma((4,)), dma((4,)), dma((4,)),
            dma((4,)), dma((4,)), dma((4,)), dma((4,)),
        ],
        compiler_params=pltpu.CompilerParams(
            collective_id=0, has_side_effects=True, vmem_limit_bytes=58 << 20
        ),
        cost_estimate=pl.CostEstimate(
            flops=4 << 30, bytes_accessed=5 << 20, transcendentals=2 << 20
        ),
    )(
        text_qkv[0, 0], segments[0], image_qkv[0, 0, 0], patch_counts[0, 0],
        image_dest[0, 0], image_offset[0, 0], output_cotangent[0, 0],
    )
    text_grad, image_grad = pl.pallas_call(
        write_out,
        name="write_out",
        out_shape=(
            jax.ShapeDtypeStruct((TOK, COLS), BF16),
            jax.ShapeDtypeStruct((IMG, COLS), BF16),
        ),
        in_specs=[vmem, vmem],
        out_specs=(hbm, hbm),
        scratch_shapes=[dma((2,))],
        compiler_params=pltpu.CompilerParams(vmem_limit_bytes=4 << 20),
    )(text_grad, image_grad)
    return text_grad[None, None], image_grad[None, None, None]


def solution(mesh):
    rows = P("enc", "llm", "sp", None)
    deep = P("enc", "llm", "sp", None, None)
    return jax.shard_map(
        body, mesh=mesh,
        in_specs=(rows, P("enc", "llm", "sp"), deep, rows, rows, rows, rows),
        out_specs=(rows, deep), check_vma=False,
    )
```

time: 64.8 us -> 55.2 us (0.85)
  Pallas kernels: 60.6 us -> 54.4 us
  local copies, waits for them, and re-layouts: 3.36 us -> 0 us
    pallas_call x1 -> x2, Pallas kernels: 60.6 us -> 54.4 us  [the longest x1 53.1 us: body(): pl.pallas_call(kernel, name='slab', out_shape=(pltpu.VMEM((TOK, COLS), BF...]
    unnamed x4 -> x0, local copies, waits for them, and re-layouts: 3.36 us -> none
where the time goes in v2:
time: 55.2 us; the launch traced here: 55.1 us
  Pallas kernels  54.4 us (99%)
  between operations  0.64 us (1%)
    pallas_call x1, Pallas kernels, body(): pl.pallas_call(kernel, name='slab', out_shape=(pltpu.VMEM((TOK, COLS), BF...  53.1 us
    pallas_call x1, Pallas kernels, body(): pl.pallas_call(write_out, name='write_out', out_shape=(jax.ShapeDtypeStru...  1.29 us

profile of v2, /device:TPU:1, one launch (start us, length us, event | category | flops | bytes accessed | tf_op | source)
XLA Modules:
  0.0 55.1 jit_solution(2608913777519513352)
XLA Ops:
  0.6 53.1 %slab.1 = (bf16[128,5120]{1,0:T(8,128)(2,1)S(1)}, bf16[64,5120]{1,0:T(8,128)(2,1)S(1)}) custom-call(bf16[128,5120]{1,0:T(8,128)(2,1)} %bitcast.9, s32[1,128]{1,0:T(1,128)} %bitcast.14, bf16[64,5120]{1,0:T(8,128)(2,1)} %bitcast.12, s32[1,2]{1,0:T(1,128)} %bitcast.15, s32[1,64]{1,0:T(1,128)} %bitcast.16, s32[1,64]{1,0:T(1,128)} %bitcast.17, ...), custom_call_target="tpu_custom_call" | custom-call | flops 4294967296 | bytes 5242880 | tf_op jit(solution)/shard_map/slab/pallas_call | solution.py:478
  53.8 1.3 %write_out.1 = (bf16[128,5120]{1,0:T(8,128)(2,1)}, bf16[64,5120]{1,0:T(8,128)(2,1)}) custom-call(bf16[128,5120]{1,0:T(8,128)(2,1)S(1)} %get-tuple-element.6.text_grad, bf16[64,5120]{1,0:T(8,128)(2,1)S(1)} %get-tuple-element.7.image_grad), custom_call_target="tpu_custom_call" | custom-call | tf_op jit(solution)/shard_map/write_out/pallas_call | solution.py:538

commit v3 on v2

--- a/solution.py
+++ b/solution.py
@@ -86,11 +86,20 @@
         p = lax.rem(me + i, PEERS)
         return p, (p // N_LLM, lax.rem(p, N_LLM), s)
 
-    def greet(i, carry):
-        pl.semaphore_signal(barrier, inc=1, device_id=peer(i)[1], device_id_type=MESH)
-        return carry
-
-    lax.fori_loop(1, PEERS, greet, 0)
+    def for_peers(action):
+        def some(n, carry):
+            for i in range(10):
+                action(n * 10 + i + 1)
+            return carry
+
+        lax.fori_loop(0, (PEERS - 2) // 10, some, 0)
+        action(PEERS - 1)
+
+    for_peers(
+        lambda i: pl.semaphore_signal(
+            barrier, inc=1, device_id=peer(i)[1], device_id_type=MESH
+        )
+    )
     for z in (down, down2, up):
         pl.semaphore_signal(barrier, inc=1, device_id=(e, l, z), device_id_type=MESH)
 
@@ -141,14 +150,13 @@
             row_out[g, :, t] = packed[:, t * 128 : (t + 1) * 128].reshape(PEERS, 16, 128)
         row_in[g, pl.ds(me, 1)] = row_out[g, pl.ds(me, 1)]
 
-    def pack_kv():
+    def pack_kv(t):
         packed = dot(
             pack[...],
-            four_tall(lambda t, b: img[:, kv_columns(2 * t + b // 2, b % 2)], (0, 1)),
-        ).astype(BF16)
-        for t in range(2):
-            kv_rows_out[t] = packed[:, t * 128 : (t + 1) * 128].reshape(PEERS, 16, 128)
-            kv_rows_in[t, pl.ds(me, 1)] = kv_rows_out[t, pl.ds(me, 1)]
+            four_tall(lambda _, b: img[:, kv_columns(2 * t + b // 2, b % 2)], (0,)),
+        )
+        kv_rows_out[t] = packed.astype(BF16).reshape(PEERS, 16, 128)
+        kv_rows_in[t, pl.ds(me, 1)] = kv_rows_out[t, pl.ds(me, 1)]
 
     def scatter(source, target, send_sem, recv_sem):
         def copy_of(i):
@@ -158,13 +166,7 @@
                 recv_sem=recv_sem, device_id=device, device_id_type=MESH,
             )
 
-        def three(n, carry):
-            for i in range(3):
-                copy_of(n * 3 + i + 1).start()
-            return carry
-
-        lax.fori_loop(0, (PEERS - 1) // 3, three, 0)
-        copy_of(PEERS - 1).start()
+        for_peers(lambda i: copy_of(i).start())
 
     def whole(source, target, send_sem, recv_sem):
         return pltpu.make_async_remote_copy(
@@ -187,11 +189,12 @@
     marks_of = (mark_out, mark_in, mark_send, mark_recv)
 
     loads[4].wait()
-    pack_kv()
+    pack_kv(0)
     loads[3].wait()
     pl.semaphore_wait(barrier, PEERS + 2)
     scatter(*marks_of)
     scatter(*kv_rows_of(0))
+    pack_kv(1)
     scatter(*kv_rows_of(1))
     seg_copies = [
         pltpu.make_async_remote_copy(
@@ -264,17 +267,17 @@
             device_id=(e, l, up), device_id_type=MESH,
         )
 
-    def far_copy(g):
+    def far_copy(g, t):
         return pltpu.make_async_remote_copy(
-            src_ref=far.at[g], dst_ref=far_in.at[g],
-            send_sem=far_send.at[g], recv_sem=far_recv.at[g],
+            src_ref=far.at[g, t], dst_ref=far_in.at[g, t],
+            send_sem=far_send.at[g, t], recv_sem=far_recv.at[g, t],
             device_id=(e, l, down), device_id_type=MESH,
         )
 
-    def pass_copy(g):
+    def pass_copy(g, t):
         return pltpu.make_async_remote_copy(
-            src_ref=pass_out.at[g], dst_ref=pass_in.at[g],
-            send_sem=pass_send.at[g], recv_sem=pass_recv.at[g],
+            src_ref=pass_out.at[g, t], dst_ref=pass_in.at[g, t],
+            send_sem=pass_send.at[g, t], recv_sem=pass_recv.at[g, t],
             device_id=(e, l, down), device_id_type=MESH,
         )
 
@@ -311,13 +314,15 @@
     next_copy(3).start()
 
     def chain(g):
-        far_copy(g).wait_recv()
-        pass_out[g] = (near[g] + far_in[g].astype(F32)).astype(BF16)
-        pass_copy(g).start()
+        for t in (1, 0):
+            far_copy(g, t).wait_recv()
+            pass_out[g, t] = (near[g, t] + far_in[g, t].astype(F32)).astype(BF16)
+            pass_copy(g, t).start()
 
     def finish(g):
-        pass_copy(g).wait_recv()
-        kv_grad[g] = (own[g] + pass_in[g].astype(F32)).astype(BF16)
+        for t in (1, 0):
+            pass_copy(g, t).wait_recv()
+            kv_grad[g, t] = (own[g, t] + pass_in[g, t].astype(F32)).astype(BF16)
 
     loads[6].wait()
 
@@ -364,14 +369,15 @@
                 target[0:TOK, both] = value[0:TOK] * far_part
                 target[TOK : 2 * TOK, both] = value[TOK : 2 * TOK]
                 target[2 * TOK : 3 * TOK, both] = value[0:TOK] * own_part
-        key_grad = dot(ds_t[...], queries[...])
-        value_grad = dot(probs_t[...], jnp.concatenate(cots, axis=0))
-        for t, grad in enumerate((key_grad, value_grad)):
-            half = slice(t * 128, (t + 1) * 128)
-            far[g, :, half] = grad[0:TOK].astype(BF16)
-            near[g, :, half] = grad[TOK : 2 * TOK]
-            own[g, :, half] = grad[2 * TOK : 3 * TOK]
-        far_copy(g).start()
+
+        def pass_down(t, grad):
+            far[g, t] = grad[0:TOK].astype(BF16)
+            near[g, t] = grad[TOK : 2 * TOK]
+            own[g, t] = grad[2 * TOK : 3 * TOK]
+            far_copy(g, t).start()
+
+        pass_down(1, dot(probs_t[...], jnp.concatenate(cots, axis=0)))
+        pass_down(0, dot(ds_t[...], queries[...]))
 
         @pl.when(g < 2)
         def _():
@@ -404,7 +410,7 @@
 
     def return_kv(t):
         rows = four_tall(
-            lambda _, b: kv_grad[2 * t + b // 2, :, b % 2 * 128 : (b % 2 + 1) * 128], (0,)
+            lambda _, b: kv_grad[2 * t + b // 2, b % 2], (0,)
         )
         kv_grads_out[t] = dot(collect[...], rows).astype(BF16).reshape(PEERS, 16, 128)
         kv_grads_in[t, pl.ds(me, 1)] = kv_grads_out[t, pl.ds(me, 1)]
@@ -432,7 +438,7 @@
     for g in range(KEY_VALUE_HEADS):
         for t in range(2):
             text_grad[:, kv_columns(g, t)] = masked(
-                kv_grad[g, :, t * 128 : (t + 1) * 128].astype(F32)
+                kv_grad[g, t].astype(F32)
             )
     lax.fori_loop(1, KEY_VALUE_HEADS, take_back, 0)
 
@@ -443,8 +449,11 @@
     def drain(g, carry):
         whole(*rows_of(g)).wait_send()
         whole(*grads_of(g)).wait_send()
-        for copy in (next_copy, relay_copy, far_copy, pass_copy):
+        for copy in (next_copy, relay_copy):
             copy(g).wait_send()
+        for t in range(2):
+            far_copy(g, t).wait_send()
+            pass_copy(g, t).wait_send()
         return carry
 
     lax.fori_loop(0, KEY_VALUE_HEADS, drain, 0)
@@ -458,8 +467,11 @@
 
 def write_out(text_grad, image_grad, text_out, image_out, sem):
     copies = [
-        pltpu.make_async_copy(text_grad, text_out, sem.at[0]),
-        pltpu.make_async_copy(image_grad, image_out, sem.at[1]),
+        pltpu.make_async_copy(
+            source.at[16 * n : 16 * n + 16], target.at[16 * n : 16 * n + 16], sem.at[i, n]
+        )
+        for i, (source, target) in enumerate(((text_grad, text_out), (image_grad, image_out)))
+        for n in range(source.shape[0] // 16)
     ]
     for copy in copies:
         copy.start()
@@ -474,7 +486,7 @@
     tiles = (KEY_VALUE_HEADS, PEERS, 2, 16, 128)
     kv_tiles = (2, PEERS, 16, 128)
     vmem = pl.BlockSpec(memory_space=pltpu.VMEM)
-    halo = (KEY_VALUE_HEADS, TOK, 256)
+    halo = (KEY_VALUE_HEADS, 2, TOK, 128)
     text_grad, image_grad = pl.pallas_call(
         kernel,
         name="slab",
@@ -523,7 +535,7 @@
             dma((PARTS,)), dma((PARTS,)), dma((PARTS,)), dma((PARTS,)),
             dma((2,)), dma((2,)),
             dma((4,)), dma((4,)), dma((4,)), dma((4,)),
-            dma((4,)), dma((4,)), dma((4,)), dma((4,)),
+            dma((4, 2)), dma((4, 2)), dma((4, 2)), dma((4, 2)),
         ],
         compiler_params=pltpu.CompilerParams(
             collective_id=0, has_side_effects=True, vmem_limit_bytes=58 << 20
@@ -544,7 +556,7 @@
         ),
         in_specs=[vmem, vmem],
         out_specs=(hbm, hbm),
-        scratch_shapes=[dma((2,))],
+        scratch_shapes=[dma((2, TOK // 16))],
         compiler_params=pltpu.CompilerParams(vmem_limit_bytes=4 << 20),
     )(text_grad, image_grad)
     return text_grad[None, None], image_grad[None, None, None]

time: 55.2 us -> 56.7 us (1.027)
  Pallas kernels: 54.4 us -> 56 us
    pallas_call x1, Pallas kernels: 53.1 us -> 54.6 us  [body(): pl.pallas_call(kernel, name='slab', out_shape=(pltpu.VMEM((TOK, COLS), BF...]
where the time goes in v3:
time: 56.7 us; the launch traced here: 56.6 us
  Pallas kernels  56 us (99%)
  between operations  0.64 us (1%)
    pallas_call x1, Pallas kernels, body(): pl.pallas_call(kernel, name='slab', out_shape=(pltpu.VMEM((TOK, COLS), BF...  54.6 us
    pallas_call x1, Pallas kernels, body(): pl.pallas_call(write_out, name='write_out', out_shape=(jax.ShapeDtypeStru...  1.4 us

profile of v3, /device:TPU:1, one launch (start us, length us, event | category | flops | bytes accessed | tf_op | source)
XLA Modules:
  0.0 56.6 jit_solution(1140062922988892267)
XLA Ops:
  0.6 54.6 %slab.1 = (bf16[128,5120]{1,0:T(8,128)(2,1)S(1)}, bf16[64,5120]{1,0:T(8,128)(2,1)S(1)}) custom-call(bf16[128,5120]{1,0:T(8,128)(2,1)} %bitcast.9, s32[1,128]{1,0:T(1,128)} %bitcast.14, bf16[64,5120]{1,0:T(8,128)(2,1)} %bitcast.12, s32[1,2]{1,0:T(1,128)} %bitcast.15, s32[1,64]{1,0:T(1,128)} %bitcast.16, s32[1,64]{1,0:T(1,128)} %bitcast.17, ...), custom_call_target="tpu_custom_call" | custom-call | flops 4294967296 | bytes 5242880 | tf_op jit(solution)/shard_map/slab/pallas_call | solution.py:490
  55.2 1.4 %write_out.1 = (bf16[128,5120]{1,0:T(8,128)(2,1)}, bf16[64,5120]{1,0:T(8,128)(2,1)}) custom-call(bf16[128,5120]{1,0:T(8,128)(2,1)S(1)} %get-tuple-element.6.text_grad, bf16[64,5120]{1,0:T(8,128)(2,1)S(1)} %get-tuple-element.7.image_grad), custom_call_target="tpu_custom_call" | custom-call | tf_op jit(solution)/shard_map/write_out/pallas_call | solution.py:550

commit v4 on v2

--- a/solution.py
+++ b/solution.py
@@ -293,7 +293,6 @@
 
     place_kv(0)
     next_copy(0).start()
-    next_copy(1).start()
     place_kv(1)
 
     tall = iota((16 * PEERS, TOK), 0)
@@ -305,10 +304,10 @@
     wide = iota((1, 4 * TOK), 1)
     collect[...] = one_hot(codes_col == lax.rem(wide, TOK) + 1 + wide // TOK * 256)
 
+    next_copy(1).start()
     relay(0)
+    relay(1)
     next_copy(2).start()
-    relay(1)
-    next_copy(3).start()
 
     def chain(g):
         far_copy(g).wait_recv()
@@ -373,9 +372,9 @@
             own[g, :, half] = grad[2 * TOK : 3 * TOK]
         far_copy(g).start()
 
-        @pl.when(g < 2)
+        @pl.when(g == 0)
         def _():
-            relay(g + 2)
+            next_copy(3).start()
 
         grads_t = dot(keys.T, ds_t[...]).astype(BF16)
         grads = [grads_t[:, h * 128 : (h + 1) * 128].T for h in range(GROUP)]
@@ -393,6 +392,10 @@
         for t in range(2):
             for b in range(4):
                 text_grad[:, q_columns(g, t, b)] = masked(grads[t * 4 + b].astype(F32))
+
+        @pl.when(g < 2)
+        def _():
+            relay(g + 2)
 
         @pl.when(g >= 2)
         def _():

time: 55.2 us -> 55.9 us (1.013)
  Pallas kernels: 54.4 us -> 55.1 us
    pallas_call x1, Pallas kernels: 53.1 us -> 53.8 us  [body(): pl.pallas_call(kernel, name='slab', out_shape=(pltpu.VMEM((TOK, COLS), BF...]
where the time goes in v4:
time: 55.9 us; the launch traced here: 55.8 us
  Pallas kernels  55.1 us (99%)
  between operations  0.64 us (1%)
    pallas_call x1, Pallas kernels, body(): pl.pallas_call(kernel, name='slab', out_shape=(pltpu.VMEM((TOK, COLS), BF...  53.8 us
    pallas_call x1, Pallas kernels, body(): pl.pallas_call(write_out, name='write_out', out_shape=(jax.ShapeDtypeStru...  1.29 us

profile of v4, /device:TPU:1, one launch (start us, length us, event | category | flops | bytes accessed | tf_op | source)
XLA Modules:
  0.0 55.8 jit_solution(7211170692611817349)
XLA Ops:
  0.6 53.8 %slab.1 = (bf16[128,5120]{1,0:T(8,128)(2,1)S(1)}, bf16[64,5120]{1,0:T(8,128)(2,1)S(1)}) custom-call(bf16[128,5120]{1,0:T(8,128)(2,1)} %bitcast.9, s32[1,128]{1,0:T(1,128)} %bitcast.14, bf16[64,5120]{1,0:T(8,128)(2,1)} %bitcast.12, s32[1,2]{1,0:T(1,128)} %bitcast.15, s32[1,64]{1,0:T(1,128)} %bitcast.16, s32[1,64]{1,0:T(1,128)} %bitcast.17, ...), custom_call_target="tpu_custom_call" | custom-call | flops 4294967296 | bytes 5242880 | tf_op jit(solution)/shard_map/slab/pallas_call | solution.py:481
  54.5 1.3 %write_out.1 = (bf16[128,5120]{1,0:T(8,128)(2,1)}, bf16[64,5120]{1,0:T(8,128)(2,1)}) custom-call(bf16[128,5120]{1,0:T(8,128)(2,1)S(1)} %get-tuple-element.6.text_grad, bf16[64,5120]{1,0:T(8,128)(2,1)S(1)} %get-tuple-element.7.image_grad), custom_call_target="tpu_custom_call" | custom-call | tf_op jit(solution)/shard_map/write_out/pallas_call | solution.py:541

commit v5 on v2

--- a/solution.py
+++ b/solution.py
@@ -158,13 +158,13 @@
                 recv_sem=recv_sem, device_id=device, device_id_type=MESH,
             )
 
-        def three(n, carry):
-            for i in range(3):
-                copy_of(n * 3 + i + 1).start()
+        def two(n, carry):
+            copy_of(PEERS // 2 - n).start()
+            copy_of(PEERS // 2 + n).start()
             return carry
 
-        lax.fori_loop(0, (PEERS - 1) // 3, three, 0)
-        copy_of(PEERS - 1).start()
+        copy_of(PEERS // 2).start()
+        lax.fori_loop(1, PEERS // 2, two, 0)
 
     def whole(source, target, send_sem, recv_sem):
         return pltpu.make_async_remote_copy(
@@ -426,7 +426,6 @@
     return_kv(0)
     chain(3)
     finish(2)
-    take_back(0, 0)
     finish(3)
     return_kv(1)
     for g in range(KEY_VALUE_HEADS):
@@ -434,7 +433,7 @@
             text_grad[:, kv_columns(g, t)] = masked(
                 kv_grad[g, :, t * 128 : (t + 1) * 128].astype(F32)
             )
-    lax.fori_loop(1, KEY_VALUE_HEADS, take_back, 0)
+    lax.fori_loop(0, KEY_VALUE_HEADS, take_back, 0)
 
     whole(*marks_of).wait_send()
     for copy in seg_copies:

time: 55.2 us -> 55 us (level)
  no operation moved by 1% of the time
where the time goes in v5:
time: 55 us; the launch traced here: 54.8 us
  Pallas kernels  54.2 us (99%)
  between operations  0.64 us (1%)
    pallas_call x1, Pallas kernels, body(): pl.pallas_call(kernel, name='slab', out_shape=(pltpu.VMEM((TOK, COLS), BF...  52.9 us
    pallas_call x1, Pallas kernels, body(): pl.pallas_call(write_out, name='write_out', out_shape=(jax.ShapeDtypeStru...  1.29 us

profile of v5, /device:TPU:1, one launch (start us, length us, event | category | flops | bytes accessed | tf_op | source)
XLA Modules:
  0.0 54.8 jit_solution(16541051415091515610)
XLA Ops:
  0.6 52.9 %slab.1 = (bf16[128,5120]{1,0:T(8,128)(2,1)S(1)}, bf16[64,5120]{1,0:T(8,128)(2,1)S(1)}) custom-call(bf16[128,5120]{1,0:T(8,128)(2,1)} %bitcast.9, s32[1,128]{1,0:T(1,128)} %bitcast.14, bf16[64,5120]{1,0:T(8,128)(2,1)} %bitcast.12, s32[1,2]{1,0:T(1,128)} %bitcast.15, s32[1,64]{1,0:T(1,128)} %bitcast.16, s32[1,64]{1,0:T(1,128)} %bitcast.17, ...), custom_call_target="tpu_custom_call" | custom-call | flops 4294967296 | bytes 5242880 | tf_op jit(solution)/shard_map/slab/pallas_call | solution.py:477
  53.5 1.3 %write_out.1 = (bf16[128,5120]{1,0:T(8,128)(2,1)}, bf16[64,5120]{1,0:T(8,128)(2,1)}) custom-call(bf16[128,5120]{1,0:T(8,128)(2,1)S(1)} %get-tuple-element.6.text_grad, bf16[64,5120]{1,0:T(8,128)(2,1)S(1)} %get-tuple-element.7.image_grad), custom_call_target="tpu_custom_call" | custom-call | tf_op jit(solution)/shard_map/write_out/pallas_call | solution.py:537

commit v6 on v5

--- a/solution.py
+++ b/solution.py
@@ -321,6 +321,20 @@
 
     loads[6].wait()
 
+    def back(g, carry):
+        grads_t = dot(kv[g, :, 0:128].T, ds_t[g]).astype(BF16)
+        grads = [grads_t[:, h * 128 : (h + 1) * 128].T for h in range(GROUP)]
+        gathered = dot(collect[...], four_tall(lambda t, b: grads[t * 4 + b], (0, 1)))
+        gathered = gathered.astype(BF16)
+        for t in range(2):
+            grad_out[g, :, t] = gathered[:, t * 128 : (t + 1) * 128].reshape(PEERS, 16, 128)
+        grad_in[g, pl.ds(me, 1)] = grad_out[g, pl.ds(me, 1)]
+        scatter(*grads_of(g))
+        for t in range(2):
+            for b in range(4):
+                text_grad[:, q_columns(g, t, b)] = masked(grads[t * 4 + b].astype(F32))
+        return carry
+
     def group(g, carry):
         whole(*rows_of(g)).wait_recv()
         arrived = jnp.concatenate(
@@ -360,11 +374,11 @@
             delta = jnp.sum(raised * grad_probs, axis=0, keepdims=True) * inverse
             probs = (raised * inverse).astype(BF16)
             ds = (raised * ((grad_probs - delta) * (inverse * SCALE))).astype(BF16)
-            for target, value in ((probs_t, probs), (ds_t, ds)):
+            for target, value in ((probs_t, probs), (ds_t.at[g], ds)):
                 target[0:TOK, both] = value[0:TOK] * far_part
                 target[TOK : 2 * TOK, both] = value[TOK : 2 * TOK]
                 target[2 * TOK : 3 * TOK, both] = value[0:TOK] * own_part
-        key_grad = dot(ds_t[...], queries[...])
+        key_grad = dot(ds_t[g], queries[...])
         value_grad = dot(probs_t[...], jnp.concatenate(cots, axis=0))
         for t, grad in enumerate((key_grad, value_grad)):
             half = slice(t * 128, (t + 1) * 128)
@@ -377,22 +391,13 @@
         def _():
             relay(g + 2)
 
-        grads_t = dot(keys.T, ds_t[...]).astype(BF16)
-        grads = [grads_t[:, h * 128 : (h + 1) * 128].T for h in range(GROUP)]
-        gathered = dot(collect[...], four_tall(lambda t, b: grads[t * 4 + b], (0, 1)))
-        gathered = gathered.astype(BF16)
-        for t in range(2):
-            grad_out[g, :, t] = gathered[:, t * 128 : (t + 1) * 128].reshape(PEERS, 16, 128)
-        grad_in[g, pl.ds(me, 1)] = grad_out[g, pl.ds(me, 1)]
-        scatter(*grads_of(g))
-
         @pl.when(g >= 1)
         def _():
             chain(g - 1)
 
-        for t in range(2):
-            for b in range(4):
-                text_grad[:, q_columns(g, t, b)] = masked(grads[t * 4 + b].astype(F32))
+        @pl.when(g < 2)
+        def _():
+            back(g, 0)
 
         @pl.when(g >= 2)
         def _():
@@ -423,8 +428,9 @@
                 ]
         return carry
 
+    lax.fori_loop(2, KEY_VALUE_HEADS, back, 0)
+    chain(3)
     return_kv(0)
-    chain(3)
     finish(2)
     finish(3)
     return_kv(1)
@@ -509,7 +515,7 @@
             pltpu.VMEM((KEY_VALUE_HEADS, KEYS, 256), BF16),
             pltpu.VMEM((GROUP * TOK, 128), BF16),
             pltpu.VMEM((KEYS, GROUP * TOK), BF16),
-            pltpu.VMEM((KEYS, GROUP * TOK), BF16),
+            pltpu.VMEM((KEY_VALUE_HEADS, KEYS, GROUP * TOK), BF16),
             pltpu.VMEM(halo, BF16),
             pltpu.VMEM(halo, F32),
             pltpu.VMEM(halo, F32),

time: 55 us -> 55.2 us (level)
  no operation moved by 1% of the time
where the time goes in v6:
time: 55.2 us; the launch traced here: 55.1 us
  Pallas kernels  54.4 us (99%)
  between operations  0.64 us (1%)
    pallas_call x1, Pallas kernels, body(): pl.pallas_call(kernel, name='slab', out_shape=(pltpu.VMEM((TOK, COLS), BF...  53.1 us
    pallas_call x1, Pallas kernels, body(): pl.pallas_call(write_out, name='write_out', out_shape=(jax.ShapeDtypeStru...  1.29 us

profile of v6, /device:TPU:1, one launch (start us, length us, event | category | flops | bytes accessed | tf_op | source)
XLA Modules:
  0.0 55.1 jit_solution(8884725738025755056)
XLA Ops:
  0.6 53.1 %slab.1 = (bf16[128,5120]{1,0:T(8,128)(2,1)S(1)}, bf16[64,5120]{1,0:T(8,128)(2,1)S(1)}) custom-call(bf16[128,5120]{1,0:T(8,128)(2,1)} %bitcast.9, s32[1,128]{1,0:T(1,128)} %bitcast.14, bf16[64,5120]{1,0:T(8,128)(2,1)} %bitcast.12, s32[1,2]{1,0:T(1,128)} %bitcast.15, s32[1,64]{1,0:T(1,128)} %bitcast.16, s32[1,64]{1,0:T(1,128)} %bitcast.17, ...), custom_call_target="tpu_custom_call" | custom-call | flops 4294967296 | bytes 5242880 | tf_op jit(solution)/shard_map/slab/pallas_call | solution.py:483
  53.8 1.3 %write_out.1 = (bf16[128,5120]{1,0:T(8,128)(2,1)}, bf16[64,5120]{1,0:T(8,128)(2,1)}) custom-call(bf16[128,5120]{1,0:T(8,128)(2,1)S(1)} %get-tuple-element.6.text_grad, bf16[64,5120]{1,0:T(8,128)(2,1)S(1)} %get-tuple-element.7.image_grad), custom_call_target="tpu_custom_call" | custom-call | tf_op jit(solution)/shard_map/write_out/pallas_call | solution.py:543
